TPU v7x, 256 devices: a whole 4x4x8 slice. The times are simulated.
256 devices in a mesh: frame: 4 (over x_lo, core), height: 8 (over z), width: 8 (over x_hi, y).
Axes of the slice: x: 4 (x_hi: 2, x_lo: 2; x = x_hi * 2 + x_lo), y: 4, z: 8, core: 2. Of those that a mesh axis runs over, the one named last changes fastest.
Arguments:
- queries: bfloat16 [16, 48, 64, 128], P('frame', 'height', 'width'), may hold values from -8 to 8
- key_vectors: bfloat16 [16, 48, 64, 128], P('frame', 'height', 'width'), may hold values from -8 to 8
- value_vectors: bfloat16 [16, 48, 64, 128], P('frame', 'height', 'width'), may hold values from -24 to 24
- out_weight: bfloat16 [128, 3072], replicated, may hold values from -0.5 to 0.5
- projected_grad: bfloat16 [16, 48, 64, 3072], P('frame', 'height', 'width'), may hold values from -6 to 6
Outputs:
- projected: bfloat16 [16, 48, 64, 3072], P('frame', 'height', 'width')
- grad_query: bfloat16 [16, 48, 64, 128], P('frame', 'height', 'width')
- grad_key: bfloat16 [16, 48, 64, 128], P('frame', 'height', 'width')
- grad_value: bfloat16 [16, 48, 64, 128], P('frame', 'height', 'width')
- grad_out_weight: float32 [128, 3072], replicated
All inputs are finite; a program needn't handle non-finite values.
Results may differ from a plain program's by a relative error of at most 0.023.
Values may be sent and summed in bfloat16 or wider, within the bound.
A program may use at most 128 MiB of HBM per device.

v0:
```python
import math

import jax
import jax.numpy as jnp
from jax import lax
from jax.sharding import PartitionSpec as P


def shifted(block, axis, distance):
    devices = range(lax.axis_size(axis))
    route = [(i - distance, i) for i in devices if i - distance in devices]
    return lax.ppermute(block, axis, route)


def window_start(position, extent):
    return jnp.maximum(jnp.minimum(position - 1, extent - 3), 0)


def near_tiles(source, axis_dim, position, extent, sender):
    tile_len = source.shape[axis_dim]
    strides = (2, 1, -1, -2)
    arrived = {stride: sender(source, stride) for stride in strides}
    blanks = jnp.zeros_like(source)
    ordered = [
        source if stride == 0 else arrived.get(stride, blanks) for stride in (2, 1, 0, -1, -2)
    ]
    joined = jnp.concatenate(ordered, axis=axis_dim)
    offset = (window_start(position, extent) - position + 2) * tile_len
    return lax.dynamic_slice_in_dim(joined, offset, min(3, extent) * tile_len, axis_dim)


def place_window(window_grads, axis_dim, start_tile, tile_len, total_tiles):
    grid_shape = list(window_grads.shape)
    grid_shape[axis_dim] = total_tiles * tile_len
    blanks = jnp.zeros(tuple(grid_shape), jnp.float32)
    return lax.dynamic_update_slice_in_dim(blanks, window_grads, start_tile * tile_len, axis_dim)


def return_near(window_grads, axis_dim, position, extent, tile_len, sender):
    placed = place_window(
        window_grads, axis_dim, window_start(position, extent) - position + 2, tile_len, 5
    )
    summed = lax.slice_in_dim(placed, 2 * tile_len, 3 * tile_len, axis=axis_dim)
    strides = (-2, -1, 1, 2)
    for stride in strides:
        piece_out = lax.slice_in_dim(
            placed, (stride + 2) * tile_len, (stride + 3) * tile_len, axis=axis_dim
        )
        summed = summed + sender(piece_out, stride)
    return summed


def fetch_frame(stacked):
    extent = lax.axis_size("frame")
    position = lax.axis_index("frame")
    return near_tiles(
        stacked, 1, position, extent, lambda incoming, stride: shifted(incoming, "frame", stride)
    )


def fetch_height(stacked):
    extent = lax.axis_size("height")
    position = lax.axis_index("height")
    return near_tiles(
        stacked, 2, position, extent, lambda incoming, stride: shifted(incoming, "height", stride)
    )


def fetch_width(stacked):
    extent = lax.axis_size("width")
    position = lax.axis_index("width")
    return near_tiles(
        stacked, 3, position, extent, lambda incoming, stride: shifted(incoming, "width", stride)
    )


def return_frame(window_grads, tile_len):
    extent = lax.axis_size("frame")
    position = lax.axis_index("frame")
    return return_near(
        window_grads,
        1,
        position,
        extent,
        tile_len,
        lambda outgoing, stride: shifted(outgoing.astype(jnp.bfloat16), "frame", stride).astype(
            outgoing.dtype
        ),
    )


def return_height(window_grads, tile_len):
    extent = lax.axis_size("height")
    position = lax.axis_index("height")
    return return_near(
        window_grads,
        2,
        position,
        extent,
        tile_len,
        lambda outgoing, stride: shifted(outgoing.astype(jnp.bfloat16), "height", stride).astype(
            outgoing.dtype
        ),
    )


def return_width(window_grads, tile_len):
    extent = lax.axis_size("width")
    position = lax.axis_index("width")
    return return_near(
        window_grads,
        3,
        position,
        extent,
        tile_len,
        lambda outgoing, stride: shifted(outgoing.astype(jnp.bfloat16), "width", stride).astype(
            outgoing.dtype
        ),
    )


def gradient_block(
    probability, prob_bf, attended_grad, row_dot, query_rows, key_rows, value_rows, inv_root
):
    prob_grad = jnp.einsum(
        "qd,kd->qk", attended_grad, value_rows, preferred_element_type=jnp.float32
    )
    score_grad = (probability * (prob_grad - row_dot)).astype(jnp.bfloat16)
    query_part = jnp.dot(score_grad, key_rows, preferred_element_type=jnp.float32)
    key_part = (
        jnp.einsum("qk,qd->kd", score_grad, query_rows, preferred_element_type=jnp.float32)
        * inv_root
    )
    value_part = jnp.einsum("qk,qd->kd", prob_bf, attended_grad, preferred_element_type=jnp.float32)
    return (query_part, key_part, value_part)


def body(queries, key_vectors, value_vectors, out_weight, projected_grad):
    frame_len, height_len, width_len, head_dim = queries.shape
    model_dim = out_weight.shape[1]
    inv_root = 1.0 / math.sqrt(head_dim)
    stacked = jnp.stack((key_vectors, value_vectors))
    window = fetch_width(fetch_height(fetch_frame(stacked)))
    key_rows = window[0].reshape(-1, head_dim)
    value_rows = window[1].reshape(-1, head_dim)
    query_rows = queries.reshape(-1, head_dim)
    grad_rows = projected_grad.reshape(-1, model_dim)
    scores = (
        jnp.einsum("qd,kd->qk", query_rows, key_rows, preferred_element_type=jnp.float32) * inv_root
    )
    row_max = jnp.max(scores, axis=1, keepdims=True)
    row_sum = jnp.sum(jnp.exp(scores - row_max), axis=1, keepdims=True)
    probability = jnp.exp(scores - row_max) / row_sum
    prob_bf = probability.astype(jnp.bfloat16)
    attended = jnp.dot(prob_bf, value_rows, preferred_element_type=jnp.float32).astype(jnp.bfloat16)
    projected = (
        jnp.dot(attended, out_weight, preferred_element_type=jnp.float32)
        .astype(jnp.bfloat16)
        .reshape(projected_grad.shape)
    )
    attended_grad = jnp.einsum(
        "tm,dm->td", grad_rows, out_weight, preferred_element_type=jnp.float32
    ).astype(jnp.bfloat16)
    weight_term = jnp.einsum("td,tm->dm", attended, grad_rows, preferred_element_type=jnp.float32)
    tile_count = lax.axis_size("frame") * lax.axis_size("height") * lax.axis_size("width")
    grad_out_weight = lax.psum(weight_term, ("frame", "height", "width")) / float(tile_count)
    row_dot = jnp.sum(
        attended_grad.astype(jnp.float32) * attended.astype(jnp.float32), axis=1, keepdims=True
    )
    slab_rows = frame_len * window.shape[2] * window.shape[3]
    query_grad = jnp.zeros((query_rows.shape[0], head_dim), jnp.float32)
    key_parts = []
    value_parts = []
    for slab_index in range(window.shape[1] // frame_len):
        key_block = key_rows[slab_index * slab_rows : (slab_index + 1) * slab_rows]
        value_block = value_rows[slab_index * slab_rows : (slab_index + 1) * slab_rows]
        block_scores = (
            jnp.einsum("qd,kd->qk", query_rows, key_block, preferred_element_type=jnp.float32)
            * inv_root
        )
        block_prob = jnp.exp(block_scores - row_max) / row_sum
        piece_query, piece_key, piece_value = gradient_block(
            block_prob,
            block_prob.astype(jnp.bfloat16),
            attended_grad,
            row_dot,
            query_rows,
            key_block,
            value_block,
            inv_root,
        )
        query_grad = query_grad + piece_query
        key_parts.append(piece_key)
        value_parts.append(piece_value)
    key_grad = jnp.concatenate(key_parts, axis=0)
    value_grad = jnp.concatenate(value_parts, axis=0)
    grad_query = (query_grad * inv_root).astype(jnp.bfloat16).reshape(queries.shape)
    window_grads = jnp.stack((key_grad, value_grad)).reshape(window.shape)
    returned = return_frame(
        return_height(return_width(window_grads, width_len), height_len), frame_len
    )
    grad_key = returned[0].astype(jnp.bfloat16)
    grad_value = returned[1].astype(jnp.bfloat16)
    return (projected, grad_query, grad_key, grad_value, grad_out_weight)


def solution(mesh):
    in_specs = (
        P("frame", "height", "width", None),
        P("frame", "height", "width", None),
        P("frame", "height", "width", None),
        P(),
        P("frame", "height", "width", None),
    )
    out_specs = (
        P("frame", "height", "width", None),
        P("frame", "height", "width", None),
        P("frame", "height", "width", None),
        P("frame", "height", "width", None),
        P(),
    )
    return jax.shard_map(body, mesh=mesh, in_specs=in_specs, out_specs=out_specs, check_vma=False)
```

profile of v0, /device:TPU:1, one launch (start us, length us, event | category | flops | bytes accessed | tf_op | source)
XLA Modules:
  0.0 466.2 jit_solution(7180162179761500376)
XLA Ops:
  7.2 0.9 pad_maximum_fusion.2
  8.1 4.0 collective-permute-start
  12.1 1.9 collective-permute-start.1
  14.0 2.4 collective-permute-start.2
  16.5 1.3 collective-permute-start.3
  17.8 0.8 constant_dynamic-update-slice_fusion.2
  18.7 1.3 collective-permute-done.2
  20.0 2.9 collective-permute-done.3
  22.9 0.7 constant_dynamic-slice_fusion.9
  23.6 5.6 %collective-permute-start.4 = (bf16[2,12,6,8,128]{4,3,2,1,0:T(8,128)(2,1)}, bf16[2,12,6,8,128]{4,3,2,1,0:T(8,128)(2,1)}, u32[]{:S(2)}, u32[]{:S(2)}) collective-permute-start(bf16[2,12,6,8,128]{4,3,2,1,0:T(8,128)(2,1)} %constant_dynamic-slice_fusion.9), channel_id=1, source_target_pairs={{0,16},{8,24},{16,32},{24,40},{32,48},{40,56},{1,17},{9,25},{17,33... | collective-permute-start | bytes 884744 | tf_op jit(solution)/shard_map/ppermute | solution.py:12
  29.2 3.5 collective-permute-start.5
  32.8 1.3 collective-permute-start.6
  34.1 1.3 collective-permute-start.7
  35.4 1.0 constant_dynamic-update-slice_fusion.9
  36.4 4.8 %collective-permute-done.5 = bf16[2,12,6,8,128]{4,3,2,1,0:T(8,128)(2,1)S(1)} collective-permute-done((bf16[2,12,6,8,128]{4,3,2,1,0:T(8,128)(2,1)}, bf16[2,12,6,8,128]{4,3,2,1,0:T(8,128)(2,1)S(1)}, u32[]{:S(2)}, u32[]{:S(2)}) %collective-permute-start.5) | collective-permute-done | bytes 294944 | tf_op jit(solution)/shard_map/ppermute | solution.py:12
  41.3 2.2 collective-permute-done.6
  43.5 13.4 %collective-permute-done.7 = bf16[2,12,6,8,128]{4,3,2,1,0:T(8,128)(2,1)S(1)} collective-permute-done((bf16[2,12,6,8,128]{4,3,2,1,0:T(8,128)(2,1)}, bf16[2,12,6,8,128]{4,3,2,1,0:T(8,128)(2,1)S(1)}, u32[]{:S(2)}, u32[]{:S(2)}) %collective-permute-start.7) | collective-permute-done | bytes 294944 | tf_op jit(solution)/shard_map/ppermute | solution.py:12
  57.0 1.0 constant_dynamic-slice_fusion.8
  58.0 5.7 %collective-permute-start.8 = (bf16[2,12,18,8,128]{4,3,2,1,0:T(8,128)(2,1)}, bf16[2,12,18,8,128]{4,3,2,1,0:T(8,128)(2,1)}, u32[]{:S(2)}, u32[]{:S(2)}) collective-permute-start(bf16[2,12,18,8,128]{4,3,2,1,0:T(8,128)(2,1)} %constant_dynamic-slice_fusion.8), channel_id=1, source_target_pairs={{0,2},{1,3},{2,4},{3,5},{4,6},{5,7},{8,10},{9,11},{10,12},{11,13},... | collective-permute-start | bytes 2654216 | tf_op jit(solution)/shard_map/ppermute | solution.py:12
  63.7 3.2 collective-permute-start.9
  66.9 1.3 collective-permute-start.10
  68.2 1.3 collective-permute-start.11
  69.5 0.5 convolution_convert_fusion.1
  70.0 10.2 %collective-permute-done.8 = bf16[2,12,18,8,128]{4,3,2,1,0:T(8,128)(2,1)} collective-permute-done((bf16[2,12,18,8,128]{4,3,2,1,0:T(8,128)(2,1)}, bf16[2,12,18,8,128]{4,3,2,1,0:T(8,128)(2,1)}, u32[]{:S(2)}, u32[]{:S(2)}) %collective-permute-start.8) | collective-permute-done | bytes 884768 | tf_op jit(solution)/shard_map/ppermute | solution.py:12
  80.2 1.3 constant_dynamic-update-slice_fusion.14
  81.5 17.6 %collective-permute-done.9 = bf16[2,12,18,8,128]{4,3,2,1,0:T(8,128)(2,1)} collective-permute-done((bf16[2,12,18,8,128]{4,3,2,1,0:T(8,128)(2,1)}, bf16[2,12,18,8,128]{4,3,2,1,0:T(8,128)(2,1)}, u32[]{:S(2)}, u32[]{:S(2)}) %collective-permute-start.9) | collective-permute-done | bytes 884768 | tf_op jit(solution)/shard_map/ppermute | solution.py:12
  99.1 1.4 constant_dynamic-update-slice_fusion.13
  100.8 37.3 %collective-permute-done.10 = bf16[2,12,18,8,128]{4,3,2,1,0:T(8,128)(2,1)} collective-permute-done((bf16[2,12,18,8,128]{4,3,2,1,0:T(8,128)(2,1)}, bf16[2,12,18,8,128]{4,3,2,1,0:T(8,128)(2,1)}, u32[]{:S(2)}, u32[]{:S(2)}) %collective-permute-start.10) | collective-permute-done | bytes 884768 | tf_op jit(solution)/shard_map/ppermute | solution.py:12
  138.1 1.4 constant_dynamic-update-slice_fusion.11
  139.5 1.4 constant_dynamic-update-slice_fusion.10
  141.7 0.8 fusion.45
  142.5 0.7 fusion
  144.4 1.1 multiply_reduce_fusion
  145.5 0.5 fusion.32
  148.1 0.5 convolution_multiply_fusion.5
  150.7 0.6 broadcast_in_dim.14
  151.2 0.6 maximum_dynamic-update-slice_fusion
  151.8 0.6 convert.26
  152.4 2.9 copy-done.1
  155.3 2.1 fusion.42
  157.3 1.3 collective-permute-start.12
  158.6 1.5 collective-permute-start.13
  160.1 5.0 %collective-permute-start.14 = (bf16[2,12,18,8,128]{4,3,2,1,0:T(8,128)(2,1)}, bf16[2,12,18,8,128]{4,3,2,1,0:T(8,128)(2,1)}, u32[]{:S(2)}, u32[]{:S(2)}) collective-permute-start(bf16[2,12,18,8,128]{4,3,2,1,0:T(8,128)(2,1)} %get-tuple-element.7), channel_id=1, source_target_pairs={{0,1},{1,2},{2,3},{3,4},{4,5},{5,6},{6,7},{8,9},{9,10},{10,11},{11... | collective-permute-start | bytes 2654216 | tf_op jit(solution)/shard_map/ppermute | solution.py:12
  165.1 5.5 %collective-permute-start.15 = (bf16[2,12,18,8,128]{4,3,2,1,0:T(8,128)(2,1)}, bf16[2,12,18,8,128]{4,3,2,1,0:T(8,128)(2,1)}, u32[]{:S(2)}, u32[]{:S(2)}) collective-permute-start(bf16[2,12,18,8,128]{4,3,2,1,0:T(8,128)(2,1)} %get-tuple-element.6), channel_id=1, source_target_pairs={{0,2},{1,3},{2,4},{3,5},{4,6},{5,7},{8,10},{9,11},{10,12},{11,13},... | collective-permute-start | bytes 2654216 | tf_op jit(solution)/shard_map/ppermute | solution.py:12
  170.5 1.6 fusion.48
  172.1 1.4 fusion.46
  173.5 1.5 convolution_convert_fusion
  175.0 4.4 collective-permute-done.12
  179.4 8.8 %collective-permute-done.13 = bf16[2,12,18,8,128]{4,3,2,1,0:T(8,128)(2,1)} collective-permute-done((bf16[2,12,18,8,128]{4,3,2,1,0:T(8,128)(2,1)}, bf16[2,12,18,8,128]{4,3,2,1,0:T(8,128)(2,1)}, u32[]{:S(2)}, u32[]{:S(2)}) %collective-permute-start.13) | collective-permute-done | bytes 884768 | tf_op jit(solution)/shard_map/ppermute | solution.py:12
  188.2 17.8 %collective-permute-done.15 = bf16[2,12,18,8,128]{4,3,2,1,0:T(8,128)(2,1)} collective-permute-done((bf16[2,12,18,8,128]{4,3,2,1,0:T(8,128)(2,1)}, bf16[2,12,18,8,128]{4,3,2,1,0:T(8,128)(2,1)}, u32[]{:S(2)}, u32[]{:S(2)}) %collective-permute-start.15) | collective-permute-done | bytes 884768 | tf_op jit(solution)/shard_map/ppermute | solution.py:12
  206.2 3.1 fusion.23
  209.6 1.4 collective-permute-start.16
  211.0 1.3 collective-permute-start.17
  212.3 4.0 collective-permute-start.18
  216.3 4.9 %collective-permute-start.19 = (bf16[2,12,6,8,128]{4,3,2,1,0:T(8,128)(2,1)S(1)}, bf16[2,12,6,8,128]{4,3,2,1,0:T(8,128)(2,1)S(1)}, u32[]{:S(2)}, u32[]{:S(2)}) collective-permute-start(bf16[2,12,6,8,128]{4,3,2,1,0:T(8,128)(2,1)S(1)} %get-tuple-element.18), channel_id=1, source_target_pairs={{0,16},{8,24},{16,32},{24,40},{32,48},{40,56},{1,17},{9,25},{17,33... | collective-permute-start | bytes 884744 | tf_op jit(solution)/shard_map/ppermute | solution.py:12
  221.6 1.0 fusion.26
  222.6 5.7 %collective-permute-done.17 = bf16[2,12,6,8,128]{4,3,2,1,0:T(8,128)(2,1)S(1)} collective-permute-done((bf16[2,12,6,8,128]{4,3,2,1,0:T(8,128)(2,1)S(1)}, bf16[2,12,6,8,128]{4,3,2,1,0:T(8,128)(2,1)S(1)}, u32[]{:S(2)}, u32[]{:S(2)}) %collective-permute-start.17) | collective-permute-done | bytes 294944 | tf_op jit(solution)/shard_map/ppermute | solution.py:12
  228.7 1.3 collective-permute-start.20
  230.0 4.0 collective-permute-start.21
  234.0 8.0 %collective-permute-start.22 = (bf16[2,4,6,8,128]{4,3,2,1,0:T(8,128)(2,1)S(1)}, bf16[2,4,6,8,128]{4,3,2,1,0:T(8,128)(2,1)S(1)}, u32[]{:S(2)}, u32[]{:S(2)}) collective-permute-start(bf16[2,4,6,8,128]{4,3,2,1,0:T(8,128)(2,1)S(1)} %get-tuple-element.23), channel_id=1, source_target_pairs={{0,64},{64,128},{128,192},{1,65},{65,129},{129,193},{2,66},{66,130... | collective-permute-start | bytes 294920 | tf_op jit(solution)/shard_map/ppermute | solution.py:12
  241.9 1.4 collective-permute-start.23
  243.3 212.5 %all-reduce.2.cloned.1.call-done = f32[128,3072]{1,0:T(8,128)} async-done(((f32[128,3072]{1,0:T(8,128)}), f32[128,3072]{1,0:T(8,128)}) %all-reduce.2.cloned.1.call-update) | async-done | bytes 1572880 | tf_op jit(solution)/shard_map/psum | solution.py:166
  455.9 2.7 broadcast_multiply_fusion
  458.7 0.6 slice_bitcast_fusion
  (65 shorter events, 7.9 us)
Async XLA Ops:
  7.2 62.3 %copy-start = (bf16[4,6,8,3072]{3,2,1,0:T(8,128)(2,1)S(1)}, bf16[4,6,8,3072]{3,2,1,0:T(8,128)(2,1)}, u32[]{:S(2)}) copy-start(bf16[4,6,8,3072]{3,2,1,0:T(8,128)(2,1)} %param.9) | copy-start | bytes 3538948
  7.2 448.7 %all-reduce.2.cloned.1.call-start = ((), (), s32[]{:S(2)}) async-start(), calls=%async_computation | async-start | bytes 3145728 | tf_op jit(solution)/shard_map/psum | solution.py:166
  8.1 9.6 %collective-permute-start = (bf16[2,4,6,8,128]{4,3,2,1,0:T(8,128)(2,1)S(1)}, bf16[2,4,6,8,128]{4,3,2,1,0:T(8,128)(2,1)S(1)}, u32[]{:S(2)}, u32[]{:S(2)}) collective-permute-start(bf16[2,4,6,8,128]{4,3,2,1,0:T(8,128)(2,1)S(1)} %pad_maximum_fusion.2), channel_id=1, source_target_pairs={{0,128},{64,192},{1,129},{65,193},{2,130},{66,194},{3,131},{67,195... | collective-permute-start | bytes 294920 | tf_op jit(solution)/shard_map/ppermute | solution.py:12
  12.1 5.7 %collective-permute-start.1 = (bf16[2,4,6,8,128]{4,3,2,1,0:T(8,128)(2,1)S(1)}, bf16[2,4,6,8,128]{4,3,2,1,0:T(8,128)(2,1)S(1)}, u32[]{:S(2)}, u32[]{:S(2)}) collective-permute-start(bf16[2,4,6,8,128]{4,3,2,1,0:T(8,128)(2,1)S(1)} %pad_maximum_fusion.2), channel_id=1, source_target_pairs={{0,64},{64,128},{128,192},{1,65},{65,129},{129,193},{2,66},{66,130... | collective-permute-start | bytes 294920 | tf_op jit(solution)/shard_map/ppermute | solution.py:12
  14.0 5.9 %collective-permute-start.2 = (bf16[2,4,6,8,128]{4,3,2,1,0:T(8,128)(2,1)S(1)}, bf16[2,4,6,8,128]{4,3,2,1,0:T(8,128)(2,1)S(1)}, u32[]{:S(2)}, u32[]{:S(2)}) collective-permute-start(bf16[2,4,6,8,128]{4,3,2,1,0:T(8,128)(2,1)S(1)} %pad_maximum_fusion.2), channel_id=1, source_target_pairs={{64,0},{128,64},{192,128},{65,1},{129,65},{193,129},{66,2},{130,66... | collective-permute-start | bytes 294920 | tf_op jit(solution)/shard_map/ppermute | solution.py:12
  16.5 6.4 %collective-permute-start.3 = (bf16[2,4,6,8,128]{4,3,2,1,0:T(8,128)(2,1)S(1)}, bf16[2,4,6,8,128]{4,3,2,1,0:T(8,128)(2,1)S(1)}, u32[]{:S(2)}, u32[]{:S(2)}) collective-permute-start(bf16[2,4,6,8,128]{4,3,2,1,0:T(8,128)(2,1)S(1)} %pad_maximum_fusion.2), channel_id=1, source_target_pairs={{128,0},{192,64},{129,1},{193,65},{130,2},{194,66},{131,3},{195,67... | collective-permute-start | bytes 294920 | tf_op jit(solution)/shard_map/ppermute | solution.py:12
  23.6 11.8 %collective-permute-start.4 = (bf16[2,12,6,8,128]{4,3,2,1,0:T(8,128)(2,1)}, bf16[2,12,6,8,128]{4,3,2,1,0:T(8,128)(2,1)}, u32[]{:S(2)}, u32[]{:S(2)}) collective-permute-start(bf16[2,12,6,8,128]{4,3,2,1,0:T(8,128)(2,1)} %constant_dynamic-slice_fusion.9), channel_id=1, source_target_pairs={{0,16},{8,24},{16,32},{24,40},{32,48},{40,56},{1,17},{9,25},{17,33... | collective-permute-start | bytes 884744 | tf_op jit(solution)/shard_map/ppermute | solution.py:12
  29.2 11.9 %collective-permute-start.5 = (bf16[2,12,6,8,128]{4,3,2,1,0:T(8,128)(2,1)}, bf16[2,12,6,8,128]{4,3,2,1,0:T(8,128)(2,1)S(1)}, u32[]{:S(2)}, u32[]{:S(2)}) collective-permute-start(bf16[2,12,6,8,128]{4,3,2,1,0:T(8,128)(2,1)} %constant_dynamic-slice_fusion.9), channel_id=1, source_target_pairs={{0,8},{8,16},{16,24},{24,32},{32,40},{40,48},{48,56},{1,9},{9,17},... | collective-permute-start | bytes 884744 | tf_op jit(solution)/shard_map/ppermute | solution.py:12
  32.8 10.7 %collective-permute-start.6 = (bf16[2,12,6,8,128]{4,3,2,1,0:T(8,128)(2,1)}, bf16[2,12,6,8,128]{4,3,2,1,0:T(8,128)(2,1)S(1)}, u32[]{:S(2)}, u32[]{:S(2)}) collective-permute-start(bf16[2,12,6,8,128]{4,3,2,1,0:T(8,128)(2,1)} %constant_dynamic-slice_fusion.9), channel_id=1, source_target_pairs={{8,0},{16,8},{24,16},{32,24},{40,32},{48,40},{56,48},{9,1},{17,9},... | collective-permute-start | bytes 884744 | tf_op jit(solution)/shard_map/ppermute | solution.py:12
  34.1 22.9 %collective-permute-start.7 = (bf16[2,12,6,8,128]{4,3,2,1,0:T(8,128)(2,1)}, bf16[2,12,6,8,128]{4,3,2,1,0:T(8,128)(2,1)S(1)}, u32[]{:S(2)}, u32[]{:S(2)}) collective-permute-start(bf16[2,12,6,8,128]{4,3,2,1,0:T(8,128)(2,1)} %constant_dynamic-slice_fusion.9), channel_id=1, source_target_pairs={{16,0},{24,8},{32,16},{40,24},{48,32},{56,40},{17,1},{25,9},{33,17... | collective-permute-start | bytes 884744 | tf_op jit(solution)/shard_map/ppermute | solution.py:12
  41.3 28.3 %copy-start.2 = (bf16[128,3072]{1,0:T(8,128)(2,1)S(1)}, bf16[128,3072]{1,0:T(8,128)(2,1)}, u32[]{:S(2)}) copy-start(bf16[128,3072]{1,0:T(8,128)(2,1)} %param.8) | copy-start | bytes 2359300
  58.0 22.2 %collective-permute-start.8 = (bf16[2,12,18,8,128]{4,3,2,1,0:T(8,128)(2,1)}, bf16[2,12,18,8,128]{4,3,2,1,0:T(8,128)(2,1)}, u32[]{:S(2)}, u32[]{:S(2)}) collective-permute-start(bf16[2,12,18,8,128]{4,3,2,1,0:T(8,128)(2,1)} %constant_dynamic-slice_fusion.8), channel_id=1, source_target_pairs={{0,2},{1,3},{2,4},{3,5},{4,6},{5,7},{8,10},{9,11},{10,12},{11,13},... | collective-permute-start | bytes 2654216 | tf_op jit(solution)/shard_map/ppermute | solution.py:12
  63.7 35.5 %collective-permute-start.9 = (bf16[2,12,18,8,128]{4,3,2,1,0:T(8,128)(2,1)}, bf16[2,12,18,8,128]{4,3,2,1,0:T(8,128)(2,1)}, u32[]{:S(2)}, u32[]{:S(2)}) collective-permute-start(bf16[2,12,18,8,128]{4,3,2,1,0:T(8,128)(2,1)} %constant_dynamic-slice_fusion.8), channel_id=1, source_target_pairs={{0,1},{1,2},{2,3},{3,4},{4,5},{5,6},{6,7},{8,9},{9,10},{10,11},{11... | collective-permute-start | bytes 2654216 | tf_op jit(solution)/shard_map/ppermute | solution.py:12
  66.9 71.2 %collective-permute-start.10 = (bf16[2,12,18,8,128]{4,3,2,1,0:T(8,128)(2,1)}, bf16[2,12,18,8,128]{4,3,2,1,0:T(8,128)(2,1)}, u32[]{:S(2)}, u32[]{:S(2)}) collective-permute-start(bf16[2,12,18,8,128]{4,3,2,1,0:T(8,128)(2,1)} %constant_dynamic-slice_fusion.8), channel_id=1, source_target_pairs={{1,0},{2,1},{3,2},{4,3},{5,4},{6,5},{7,6},{9,8},{10,9},{11,10},{12... | collective-permute-start | bytes 2654216 | tf_op jit(solution)/shard_map/ppermute | solution.py:12
  68.2 71.3 %collective-permute-start.11 = (bf16[2,12,18,8,128]{4,3,2,1,0:T(8,128)(2,1)}, bf16[2,12,18,8,128]{4,3,2,1,0:T(8,128)(2,1)}, u32[]{:S(2)}, u32[]{:S(2)}) collective-permute-start(bf16[2,12,18,8,128]{4,3,2,1,0:T(8,128)(2,1)} %constant_dynamic-slice_fusion.8), channel_id=1, source_target_pairs={{2,0},{3,1},{4,2},{5,3},{6,4},{7,5},{10,8},{11,9},{12,10},{13,11},... | collective-permute-start | bytes 2654216 | tf_op jit(solution)/shard_map/ppermute | solution.py:12
  140.9 0.8 copy-start.9
  143.6 0.8 copy-start.7
  143.7 3.2 copy-start.6
  143.7 4.9 %copy-start.4 = (bf16[1,4,18,24,128]{4,3,2,1,0:T(8,128)(2,1)}, bf16[1,4,18,24,128]{4,3,2,1,0:T(8,128)(2,1)S(1)}, u32[]{:S(2)}) copy-start(bf16[1,4,18,24,128]{4,3,2,1,0:T(8,128)(2,1)S(1)} %get-tuple-element.10) | copy-start | bytes 1327108
  151.8 3.4 copy-start.1
  157.3 22.1 %collective-permute-start.12 = (bf16[2,12,18,8,128]{4,3,2,1,0:T(8,128)(2,1)}, bf16[2,12,18,8,128]{4,3,2,1,0:T(8,128)(2,1)}, u32[]{:S(2)}, u32[]{:S(2)}) collective-permute-start(bf16[2,12,18,8,128]{4,3,2,1,0:T(8,128)(2,1)} %get-tuple-element.5), channel_id=1, source_target_pairs={{2,0},{3,1},{4,2},{5,3},{6,4},{7,5},{10,8},{11,9},{12,10},{13,11},... | collective-permute-start | bytes 2654216 | tf_op jit(solution)/shard_map/ppermute | solution.py:12
  158.6 29.6 %collective-permute-start.13 = (bf16[2,12,18,8,128]{4,3,2,1,0:T(8,128)(2,1)}, bf16[2,12,18,8,128]{4,3,2,1,0:T(8,128)(2,1)}, u32[]{:S(2)}, u32[]{:S(2)}) collective-permute-start(bf16[2,12,18,8,128]{4,3,2,1,0:T(8,128)(2,1)} %get-tuple-element.8), channel_id=1, source_target_pairs={{1,0},{2,1},{3,2},{4,3},{5,4},{6,5},{7,6},{9,8},{10,9},{11,10},{12... | collective-permute-start | bytes 2654216 | tf_op jit(solution)/shard_map/ppermute | solution.py:12
  160.1 28.1 %collective-permute-start.14 = (bf16[2,12,18,8,128]{4,3,2,1,0:T(8,128)(2,1)}, bf16[2,12,18,8,128]{4,3,2,1,0:T(8,128)(2,1)}, u32[]{:S(2)}, u32[]{:S(2)}) collective-permute-start(bf16[2,12,18,8,128]{4,3,2,1,0:T(8,128)(2,1)} %get-tuple-element.7), channel_id=1, source_target_pairs={{0,1},{1,2},{2,3},{3,4},{4,5},{5,6},{6,7},{8,9},{9,10},{10,11},{11... | collective-permute-start | bytes 2654216 | tf_op jit(solution)/shard_map/ppermute | solution.py:12
  165.1 41.0 %collective-permute-start.15 = (bf16[2,12,18,8,128]{4,3,2,1,0:T(8,128)(2,1)}, bf16[2,12,18,8,128]{4,3,2,1,0:T(8,128)(2,1)}, u32[]{:S(2)}, u32[]{:S(2)}) collective-permute-start(bf16[2,12,18,8,128]{4,3,2,1,0:T(8,128)(2,1)} %get-tuple-element.6), channel_id=1, source_target_pairs={{0,2},{1,3},{2,4},{3,5},{4,6},{5,7},{8,10},{9,11},{10,12},{11,13},... | collective-permute-start | bytes 2654216 | tf_op jit(solution)/shard_map/ppermute | solution.py:12
  172.1 1.4 copy-start.3
  209.5 11.8 %copy-start.5 = (bf16[1,4,18,24,128]{4,3,2,1,0:T(8,128)(2,1)S(1)}, bf16[1,4,18,24,128]{4,3,2,1,0:T(8,128)(2,1)}, u32[]{:S(2)}) copy-start(bf16[1,4,18,24,128]{4,3,2,1,0:T(8,128)(2,1)} %copy-done.4) | copy-start | bytes 1327108
  209.5 12.1 %copy-start.8 = (bf16[1,4,18,24,128]{4,3,2,1,0:T(8,128)(2,1)S(1)}, bf16[1,4,18,24,128]{4,3,2,1,0:T(8,128)(2,1)}, u32[]{:S(2)}) copy-start(bf16[1,4,18,24,128]{4,3,2,1,0:T(8,128)(2,1)} %copy-done.7) | copy-start | bytes 1327108
  209.6 13.0 %collective-permute-start.16 = (bf16[2,12,6,8,128]{4,3,2,1,0:T(8,128)(2,1)S(1)}, bf16[2,12,6,8,128]{4,3,2,1,0:T(8,128)(2,1)S(1)}, u32[]{:S(2)}, u32[]{:S(2)}) collective-permute-start(bf16[2,12,6,8,128]{4,3,2,1,0:T(8,128)(2,1)S(1)} %get-tuple-element.17), channel_id=1, source_target_pairs={{16,0},{24,8},{32,16},{40,24},{48,32},{56,40},{17,1},{25,9},{33,17... | collective-permute-start | bytes 884744 | tf_op jit(solution)/shard_map/ppermute | solution.py:12
  211.0 17.3 %collective-permute-start.17 = (bf16[2,12,6,8,128]{4,3,2,1,0:T(8,128)(2,1)S(1)}, bf16[2,12,6,8,128]{4,3,2,1,0:T(8,128)(2,1)S(1)}, u32[]{:S(2)}, u32[]{:S(2)}) collective-permute-start(bf16[2,12,6,8,128]{4,3,2,1,0:T(8,128)(2,1)S(1)} %get-tuple-element.20), channel_id=1, source_target_pairs={{8,0},{16,8},{24,16},{32,24},{40,32},{48,40},{56,48},{9,1},{17,9},... | collective-permute-start | bytes 884744 | tf_op jit(solution)/shard_map/ppermute | solution.py:12
  212.3 16.0 %collective-permute-start.18 = (bf16[2,12,6,8,128]{4,3,2,1,0:T(8,128)(2,1)S(1)}, bf16[2,12,6,8,128]{4,3,2,1,0:T(8,128)(2,1)S(1)}, u32[]{:S(2)}, u32[]{:S(2)}) collective-permute-start(bf16[2,12,6,8,128]{4,3,2,1,0:T(8,128)(2,1)S(1)} %get-tuple-element.19), channel_id=1, source_target_pairs={{0,8},{8,16},{16,24},{24,32},{32,40},{40,48},{48,56},{1,9},{9,17},... | collective-permute-start | bytes 884744 | tf_op jit(solution)/shard_map/ppermute | solution.py:12
  216.3 11.9 %collective-permute-start.19 = (bf16[2,12,6,8,128]{4,3,2,1,0:T(8,128)(2,1)S(1)}, bf16[2,12,6,8,128]{4,3,2,1,0:T(8,128)(2,1)S(1)}, u32[]{:S(2)}, u32[]{:S(2)}) collective-permute-start(bf16[2,12,6,8,128]{4,3,2,1,0:T(8,128)(2,1)S(1)} %get-tuple-element.18), channel_id=1, source_target_pairs={{0,16},{8,24},{16,32},{24,40},{32,48},{40,56},{1,17},{9,25},{17,33... | collective-permute-start | bytes 884744 | tf_op jit(solution)/shard_map/ppermute | solution.py:12
  228.7 229.9 %collective-permute-start.20 = (bf16[2,4,6,8,128]{4,3,2,1,0:T(8,128)(2,1)S(1)}, bf16[2,4,6,8,128]{4,3,2,1,0:T(8,128)(2,1)S(1)}, u32[]{:S(2)}, u32[]{:S(2)}) collective-permute-start(bf16[2,4,6,8,128]{4,3,2,1,0:T(8,128)(2,1)S(1)} %get-tuple-element.21), channel_id=1, source_target_pairs={{128,0},{192,64},{129,1},{193,65},{130,2},{194,66},{131,3},{195,67... | collective-permute-start | bytes 294920 | tf_op jit(solution)/shard_map/ppermute | solution.py:12
  230.0 228.6 %collective-permute-start.21 = (bf16[2,4,6,8,128]{4,3,2,1,0:T(8,128)(2,1)S(1)}, bf16[2,4,6,8,128]{4,3,2,1,0:T(8,128)(2,1)S(1)}, u32[]{:S(2)}, u32[]{:S(2)}) collective-permute-start(bf16[2,4,6,8,128]{4,3,2,1,0:T(8,128)(2,1)S(1)} %get-tuple-element.24), channel_id=1, source_target_pairs={{64,0},{128,64},{192,128},{65,1},{129,65},{193,129},{66,2},{130,66... | collective-permute-start | bytes 294920 | tf_op jit(solution)/shard_map/ppermute | solution.py:12
  234.0 224.6 %collective-permute-start.22 = (bf16[2,4,6,8,128]{4,3,2,1,0:T(8,128)(2,1)S(1)}, bf16[2,4,6,8,128]{4,3,2,1,0:T(8,128)(2,1)S(1)}, u32[]{:S(2)}, u32[]{:S(2)}) collective-permute-start(bf16[2,4,6,8,128]{4,3,2,1,0:T(8,128)(2,1)S(1)} %get-tuple-element.23), channel_id=1, source_target_pairs={{0,64},{64,128},{128,192},{1,65},{65,129},{129,193},{2,66},{66,130... | collective-permute-start | bytes 294920 | tf_op jit(solution)/shard_map/ppermute | solution.py:12
  241.9 216.7 %collective-permute-start.23 = (bf16[2,4,6,8,128]{4,3,2,1,0:T(8,128)(2,1)S(1)}, bf16[2,4,6,8,128]{4,3,2,1,0:T(8,128)(2,1)S(1)}, u32[]{:S(2)}, u32[]{:S(2)}) collective-permute-start(bf16[2,4,6,8,128]{4,3,2,1,0:T(8,128)(2,1)S(1)} %get-tuple-element.22), channel_id=1, source_target_pairs={{0,128},{64,192},{1,129},{65,193},{2,130},{66,194},{3,131},{67,195... | collective-permute-start | bytes 294920 | tf_op jit(solution)/shard_map/ppermute | solution.py:12
Sparse Core Ops, SparseCore 0:
  172.2 283.6 all-reduce.1
where the time goes:
time: 468 us; the launch traced here: 466 us
  waiting for transfers between devices  339 us (72%)
  starting transfers between devices  72.3 us (15%)
  local copies, waits for them, and re-layouts  16.7 us (4%)
  between operations  14.7 us (3%)
  matrix products  13.2 us (3%)
  other arithmetic  10.2 us (2%)
    psum x1, waiting for transfers between devices, body(): lax.psum(weight_term, ('frame', 'height', 'width')) / float(tile_count)  213 us
    ppermute x24, waiting for transfers between devices, shifted(): return lax.ppermute(block, axis, route)  127 us
    ppermute x24, starting transfers between devices, shifted(): return lax.ppermute(block, axis, route)  72.2 us
  transfers between devices with their start and end apart: 25, of which 13 were waited for; matrix products, arithmetic and copies ran while one was open for 4% of the time, Pallas kernels for 0%

commit v1 on v0

v1 whole, which is shorter than its diff:
```python
import functools
import math

import jax
import jax.experimental.pallas as pl
import jax.experimental.pallas.tpu as pltpu
import jax.numpy as jnp
from jax import lax
from jax.sharding import PartitionSpec as P

MESH = pl.DeviceIdType.MESH
ROWS = 192
DIM = 128
LIMIT = 56 * 2**20


class Place:
    def __init__(self):
        self.f = lax.axis_index("frame")
        self.h = lax.axis_index("height")
        self.w = lax.axis_index("width")
        self.xlo = self.f // 2
        self.core = self.f - 2 * self.xlo
        self.xhi = self.w // 4
        self.y = self.w - 4 * self.xhi
        self.ring = (2 * self.xhi + self.xlo) * 4 + self.y
        self.sibling = (self.xlo * 2 + 1 - self.core, self.h, self.w)
        self.partner = ((1 - self.xlo) * 2 + self.core, self.h, self.w)
        self.own_plane = self.f - self.xlo
        self.sib_plane = self.xlo * 2 + 1 - self.core - self.xlo
        self.third_plane = 2 * (1 - self.xlo)
        self.collects = self.core == self.xlo
        self.supplies = self.core != self.xlo
        self.hslot = self.h - start(self.h)
        self.wslot = self.w - start(self.w)

    def plane_chip(self, index):
        x = index // 4
        y = index - 4 * x
        xhi = x // 2
        return ((x - 2 * xhi) * 2 + self.core, self.h, xhi * 4 + y)


def start(index):
    return jnp.maximum(jnp.minimum(index - 1, 5), 0)


def neighbours(index):
    return (
        (index >= 1, index - 1),
        (index <= 6, index + 1),
        ((index == 2) | (index == 5), 7 * (index // 5)),
    )


def owners(index):
    return (
        (index >= 1, index - 1),
        (index <= 6, index + 1),
        ((index == 0) | (index == 7), 2 + 3 * (index // 7)),
    )


def remote(src, dst, send_sem, recv_sem, target):
    return pltpu.make_async_remote_copy(
        src_ref=src,
        dst_ref=dst,
        send_sem=send_sem,
        recv_sem=recv_sem,
        device_id=target,
        device_id_type=MESH,
    )


def arrived(ref, sem):
    pltpu.make_async_copy(ref, ref, sem).wait()


def greet_plane(place, barrier):
    def one(k, carry):
        target = place.plane_chip(lax.rem(place.ring + k, 16))
        pl.semaphore_signal(barrier, inc=1, device_id=target, device_id_type=MESH)
        return carry

    lax.fori_loop(1, 16, one, 0)


def greet_column(place, barrier):
    def one(k, carry):
        target = (place.f, lax.rem(place.h + k, 8), place.w)
        pl.semaphore_signal(barrier, inc=1, device_id=target, device_id_type=MESH)
        return carry

    lax.fori_loop(1, 8, one, 0)


def greet_all(place):
    barrier = pltpu.get_barrier_semaphore()
    pl.semaphore_signal(barrier, inc=1, device_id=place.sibling, device_id_type=MESH)
    greet_plane(place, barrier)
    greet_column(place, barrier)
    pl.semaphore_wait(barrier, 23)


def gather_kernel(k_ref, v_ref, kv, hsend, wsend, ssend, tsend, xsend, recv):
    place = Place()
    greet_all(place)
    own = place.own_plane * 9
    third = place.third_plane * 9

    kv[own + place.wslot * 3 + place.hslot, 0] = k_ref[...]
    kv[own + place.wslot * 3 + place.hslot, 1] = v_ref[...]

    def along_height():
        slot = own + place.wslot * 3 + place.hslot
        for i, (there, h) in enumerate(neighbours(place.h)):
            to = own + place.wslot * 3 + place.h - start(h)
            yield there, remote(
                kv.at[slot], kv.at[to], hsend.at[i], recv.at[to], (place.f, h, place.w)
            )

    def along_width(hslot):
        slot = own + place.wslot * 3 + hslot
        for i, (there, w) in enumerate(neighbours(place.w)):
            to = own + (place.w - start(w)) * 3 + hslot
            yield there, remote(
                kv.at[slot], kv.at[to], wsend.at[i, hslot], recv.at[to], (place.f, place.h, w)
            )

    def along_frame(tile):
        slot = own + tile
        to = 18 * place.xlo + tile
        yield True, remote(kv.at[slot], kv.at[slot], ssend.at[tile], recv.at[slot], place.sibling)
        yield (
            place.supplies,
            remote(kv.at[slot], kv.at[to], xsend.at[tile], recv.at[to], place.partner),
        )

    def third_on(tile):
        slot = third + tile
        yield (
            place.collects,
            remote(kv.at[slot], kv.at[slot], tsend.at[tile], recv.at[slot], place.sibling),
        )

    def begin(copies):
        for there, copy in copies:
            if there is True:
                copy.start()
            else:
                pl.when(there)(copy.start)

    def finish(copies):
        for there, copy in copies:
            if there is True:
                copy.wait_send()
            else:
                pl.when(there)(copy.wait_send)

    hslots = (place.hslot, lax.rem(place.hslot + 1, 3), lax.rem(place.hslot + 2, 3))
    wslots = (place.wslot, lax.rem(place.wslot + 1, 3), lax.rem(place.wslot + 2, 3))
    begin(along_height())
    begin(along_width(hslots[0]))
    begin(along_frame(wslots[0] * 3 + hslots[0]))
    for hslot in hslots[1:]:
        slot = own + wslots[0] * 3 + hslot
        arrived(kv.at[slot], recv.at[slot])
        begin(along_width(hslot))
        begin(along_frame(wslots[0] * 3 + hslot))
    for hslot in hslots:
        for wslot in wslots[1:]:
            slot = own + wslot * 3 + hslot
            arrived(kv.at[slot], recv.at[slot])
            begin(along_frame(wslot * 3 + hslot))
    for wslot in wslots:
        for hslot in hslots:
            slot = third + wslot * 3 + hslot
            arrived(kv.at[slot], recv.at[slot])
            begin(third_on(wslot * 3 + hslot))

    def from_sibling(tile, carry):
        slot = place.sib_plane * 9 + tile
        arrived(kv.at[slot], recv.at[slot])
        finish(along_frame(tile))
        finish(third_on(tile))
        return carry

    lax.fori_loop(0, 9, from_sibling, 0)
    finish(along_height())
    for hslot in range(3):
        finish(along_width(hslot))


def gather(keys, values):
    return pl.pallas_call(
        gather_kernel,
        out_shape=jax.ShapeDtypeStruct((27, 2, ROWS, DIM), jnp.bfloat16),
        in_specs=[pl.BlockSpec(memory_space=pltpu.VMEM)] * 2,
        out_specs=pl.BlockSpec(memory_space=pltpu.VMEM),
        scratch_shapes=[
            pltpu.SemaphoreType.DMA((3,)),
            pltpu.SemaphoreType.DMA((3, 3)),
            pltpu.SemaphoreType.DMA((9,)),
            pltpu.SemaphoreType.DMA((9,)),
            pltpu.SemaphoreType.DMA((9,)),
            pltpu.SemaphoreType.DMA((27,)),
        ],
        compiler_params=pltpu.CompilerParams(
            collective_id=0, has_side_effects=True, vmem_limit_bytes=LIMIT
        ),
        name="gather",
    )(keys, values)


def combine_kernel(
    parts,
    weight,
    kv_out,
    weight_out,
    half,
    pieces,
    lines,
    full,
    swap,
    third,
    cross,
    outgoing,
    wide,
    high,
    half_sem,
    piece_send,
    piece_recv,
    line_send,
    line_recv,
    full_send,
    pass_send,
    full_recv,
    swap_send,
    swap_recv,
    third_send,
    third_recv,
    cross_send,
    cross_recv,
    wide_send,
    wide_recv,
    high_send,
    high_recv,
):
    place = Place()
    greet_all(place)
    core, ring, h = place.core, place.ring, place.h
    own, sib, far = place.own_plane * 9, place.sib_plane * 9, place.third_plane * 9
    f32 = jnp.float32

    half_copy = remote(
        weight.at[1 - core], half, half_sem.at[0], half_sem.at[1], place.sibling
    )
    half_copy.start()

    def swap_copy(tile):
        return remote(
            parts.at[sib + tile], swap.at[tile], swap_send.at[tile], swap_recv.at[tile],
            place.sibling,
        )

    def third_copy(tile):
        return remote(
            parts.at[far + tile], third.at[tile], third_send.at[tile], third_recv.at[tile],
            place.sibling,
        )

    def cross_copy(tile):
        return remote(
            third.at[tile], cross.at[tile], cross_send.at[tile], cross_recv.at[tile],
            place.partner,
        )

    def start_third(tile, carry):
        third_copy(tile).start()
        return carry

    def start_swap(tile, carry):
        swap_copy(tile).start()
        return carry

    @pl.when(place.supplies)
    def _():
        lax.fori_loop(0, 9, start_third, 0)

    lax.fori_loop(0, 9, start_swap, 0)

    half_copy.wait()

    def add_half(piece, carry):
        rows = pl.ds(pl.multiple_of(piece * 96, 96), 96)
        half[rows] = (weight[core, rows].astype(f32) + half[rows].astype(f32)).astype(
            jnp.bfloat16
        )
        return carry

    lax.fori_loop(0, 16, add_half, 0)

    def piece_copy(k):
        to = lax.rem(ring + k, 16)
        rows = pl.ds(pl.multiple_of(to * 96, 96), 96)
        return remote(
            half.at[rows], pieces.at[ring], piece_send.at[to], piece_recv.at[ring],
            place.plane_chip(to),
        )

    def start_piece(k, carry):
        piece_copy(k).start()
        return carry

    lax.fori_loop(1, 16, start_piece, 0)

    @pl.when(place.collects)
    def _():
        def one(tile, carry):
            arrived(third.at[tile], third_recv.at[tile])
            third[tile] = (parts[far + tile].astype(f32) + third[tile].astype(f32)).astype(
                jnp.bfloat16
            )
            cross_copy(tile).start()
            return carry

        lax.fori_loop(0, 9, one, 0)

    mine = pl.ds(pl.multiple_of(ring * 96, 96), 96)

    def add_piece(k, total):
        other = lax.rem(ring + k, 16)
        arrived(pieces.at[other], piece_recv.at[other])
        return total + pieces[other].astype(f32)

    total = lax.fori_loop(1, 16, add_piece, half[mine].astype(f32))
    lines[h] = total.astype(jnp.bfloat16)

    def line_copy(k):
        to = lax.rem(h + k, 8)
        return remote(
            lines.at[h], lines.at[h], line_send.at[to], line_recv.at[h],
            (place.f, to, place.w),
        )

    def start_line(k, carry):
        line_copy(k).start()
        return carry

    lax.fori_loop(1, 8, start_line, 0)

    def own_tile(tile):
        arrived(swap.at[tile], swap_recv.at[tile])
        outgoing[tile] = parts[own + tile].astype(f32) + swap[tile].astype(f32)

        @pl.when(place.supplies)
        def _():
            arrived(cross.at[tile], cross_recv.at[tile])
            outgoing[tile] += cross[tile].astype(f32)

        swap[tile] = outgoing[tile].astype(jnp.bfloat16)

    def width_copy(i, w, hslot):
        tile = (w - start(place.w)) * 3 + hslot
        back = (1, 0, 2)[i]
        return remote(
            swap.at[tile], wide.at[back, hslot], wide_send.at[i, hslot],
            wide_recv.at[back, hslot], (place.f, h, w),
        )

    for i, (there, w) in enumerate(owners(place.w)):

        @pl.when(there)
        def _():
            def one(hslot, carry):
                own_tile((w - start(place.w)) * 3 + hslot)
                width_copy(i, w, hslot).start()
                return carry

            lax.fori_loop(0, 3, one, 0)

    def add_line(k, total):
        other = lax.rem(h + k, 8)
        arrived(lines.at[other], line_recv.at[other])
        return total + lines[other].astype(f32)

    total = lax.fori_loop(1, 8, add_line, total)
    full[core, mine] = (total * (1.0 / 256.0)).astype(jnp.bfloat16)

    def full_copy(k):
        to = lax.rem(ring + k, 16)
        return remote(
            full.at[core, mine], full.at[core, mine], full_send.at[to], full_recv.at[core, ring],
            place.plane_chip(to),
        )

    def pass_copy(piece):
        rows = pl.ds(pl.multiple_of(piece * 96, 96), 96)
        return remote(
            full.at[core, rows], full.at[core, rows], pass_send.at[piece],
            full_recv.at[core, piece], place.sibling,
        )

    def start_full(k, carry):
        full_copy(k).start()
        return carry

    lax.fori_loop(1, 16, start_full, 0)
    pass_copy(ring).start()

    def own_column(hslot, carry):
        own_tile(place.wslot * 3 + hslot)
        return carry

    lax.fori_loop(0, 3, own_column, 0)
    for i, (there, _w) in enumerate(neighbours(place.w)):

        @pl.when(there)
        def _():
            def one(hslot, carry):
                arrived(wide.at[i, hslot], wide_recv.at[i, hslot])
                outgoing[place.wslot * 3 + hslot] += wide[i, hslot].astype(f32)
                return carry

            lax.fori_loop(0, 3, one, 0)

    def height_copy(i, to):
        hslot = to - start(h)
        back = (1, 0, 2)[i]
        return remote(
            swap.at[place.wslot * 3 + hslot], high.at[back], high_send.at[i],
            high_recv.at[back], (place.f, to, place.w),
        )

    for i, (there, to) in enumerate(owners(h)):

        @pl.when(there)
        def _():
            tile = place.wslot * 3 + to - start(h)
            swap[tile] = outgoing[tile].astype(jnp.bfloat16)
            height_copy(i, to).start()

    def pass_on(k, carry):
        other = lax.rem(ring + k, 16)
        rows = pl.ds(pl.multiple_of(other * 96, 96), 96)
        arrived(full.at[core, rows], full_recv.at[core, other])
        pass_copy(other).start()
        return carry

    lax.fori_loop(1, 16, pass_on, 0)

    tile = place.wslot * 3 + place.hslot
    for i, (there, _h) in enumerate(neighbours(h)):

        @pl.when(there)
        def _():
            arrived(high.at[i], high_recv.at[i])
            outgoing[tile] += high[i].astype(f32)

    kv_out[...] = outgoing[tile].astype(jnp.bfloat16)

    def take_rest(piece, carry):
        rows = pl.ds(pl.multiple_of(piece * 96, 96), 96)
        arrived(full.at[1 - core, rows], full_recv.at[1 - core, piece])
        return carry

    lax.fori_loop(0, 16, take_rest, 0)
    for side in range(2):
        for block in range(12):
            weight_out[:, (side * 12 + block) * 128 : (side * 12 + block + 1) * 128] = full[
                side, block * 128 : (block + 1) * 128
            ].astype(f32)

    def left_plane(k, carry):
        piece_copy(k).wait_send()
        full_copy(k).wait_send()
        return carry

    lax.fori_loop(1, 16, left_plane, 0)

    def left_line(k, carry):
        line_copy(k).wait_send()
        return carry

    lax.fori_loop(1, 8, left_line, 0)

    def left_pass(piece, carry):
        pass_copy(piece).wait_send()
        return carry

    lax.fori_loop(0, 16, left_pass, 0)

    def left_tile(tile, carry):
        swap_copy(tile).wait_send()
        pl.when(place.supplies)(third_copy(tile).wait_send)
        pl.when(place.collects)(cross_copy(tile).wait_send)
        return carry

    lax.fori_loop(0, 9, left_tile, 0)
    for i, (there, w) in enumerate(owners(place.w)):
        for hslot in range(3):
            pl.when(there)(width_copy(i, w, hslot).wait_send)
    for i, (there, to) in enumerate(owners(h)):
        pl.when(there)(height_copy(i, to).wait_send)


def combine(parts, weight):
    bf16, f32 = jnp.bfloat16, jnp.float32
    vmem, dma = pltpu.VMEM, pltpu.SemaphoreType.DMA
    return pl.pallas_call(
        combine_kernel,
        out_shape=(
            jax.ShapeDtypeStruct((2, ROWS, DIM), bf16),
            jax.ShapeDtypeStruct((DIM, 3072), f32),
        ),
        in_specs=[pl.BlockSpec(memory_space=pltpu.VMEM)] * 2,
        out_specs=[pl.BlockSpec(memory_space=pltpu.VMEM)] * 2,
        scratch_shapes=[
            vmem((1536, DIM), bf16),
            vmem((16, 96, DIM), bf16),
            vmem((8, 96, DIM), bf16),
            vmem((2, 1536, DIM), bf16),
            vmem((9, 2, ROWS, DIM), bf16),
            vmem((9, 2, ROWS, DIM), bf16),
            vmem((9, 2, ROWS, DIM), bf16),
            vmem((9, 2, ROWS, DIM), f32),
            vmem((3, 3, 2, ROWS, DIM), bf16),
            vmem((3, 2, ROWS, DIM), bf16),
            dma((2,)),
            dma((16,)),
            dma((16,)),
            dma((8,)),
            dma((8,)),
            dma((16,)),
            dma((16,)),
            dma((2, 16)),
            dma((9,)),
            dma((9,)),
            dma((9,)),
            dma((9,)),
            dma((9,)),
            dma((9,)),
            dma((3, 3)),
            dma((3, 3)),
            dma((3,)),
            dma((3,)),
        ],
        compiler_params=pltpu.CompilerParams(
            collective_id=1, has_side_effects=True, vmem_limit_bytes=LIMIT
        ),
        name="combine",
    )(parts, weight)


def body(queries, key_vectors, value_vectors, out_weight, projected_grad):
    f32, bf16 = jnp.float32, jnp.bfloat16
    model_dim = out_weight.shape[1]
    inv_root = 1.0 / math.sqrt(DIM)
    dot = functools.partial(jnp.einsum, preferred_element_type=f32)
    window = gather(key_vectors.reshape(ROWS, DIM), value_vectors.reshape(ROWS, DIM))
    key_rows = window[:, 0].reshape(-1, DIM)
    value_rows = window[:, 1].reshape(-1, DIM)
    query_rows = queries.reshape(-1, DIM)
    grad_rows = projected_grad.reshape(-1, model_dim)
    scores = dot("qd,kd->qk", query_rows, key_rows) * inv_root
    row_max = jnp.max(scores, axis=1, keepdims=True)
    weights = jnp.exp(scores - row_max)
    probability = weights / jnp.sum(weights, axis=1, keepdims=True)
    prob_bf = probability.astype(bf16)
    attended = dot("qk,kd->qd", prob_bf, value_rows).astype(bf16)
    projected = dot("qd,dm->qm", attended, out_weight).astype(bf16)
    attended_grad = dot("tm,dm->td", grad_rows, out_weight).astype(bf16)
    weight_term = dot("td,tm->dm", attended, grad_rows).astype(bf16)
    row_dot = jnp.sum(attended_grad.astype(f32) * attended.astype(f32), axis=1, keepdims=True)
    prob_grad = dot("qd,kd->qk", attended_grad, value_rows)
    score_grad = (probability * (prob_grad - row_dot)).astype(bf16)
    grad_query = (dot("qk,kd->qd", score_grad, key_rows) * inv_root).astype(bf16)
    key_part = (dot("qk,qd->kd", score_grad, query_rows) * inv_root).astype(bf16)
    value_part = dot("qk,qd->kd", prob_bf, attended_grad).astype(bf16)
    parts = jnp.stack(
        (key_part.reshape(27, ROWS, DIM), value_part.reshape(27, ROWS, DIM)), axis=1
    )
    halves = weight_term.reshape(DIM, 2, 12, 128).transpose(1, 2, 0, 3).reshape(2, 1536, 128)
    kv_grad, grad_out_weight = combine(parts, halves)
    return (
        projected.reshape(projected_grad.shape),
        grad_query.reshape(queries.shape),
        kv_grad[0].reshape(queries.shape),
        kv_grad[1].reshape(queries.shape),
        grad_out_weight,
    )


def solution(mesh):
    spec = P("frame", "height", "width", None)
    return jax.shard_map(
        body,
        mesh=mesh,
        in_specs=(spec, spec, spec, P(), spec),
        out_specs=(spec, spec, spec, spec, P()),
        check_vma=False,
    )
```

time: 468 us -> 94.4 us (0.20)
  waiting for transfers between devices: 339 us -> 0 us
  Pallas kernels: 0 us -> 72.9 us
  starting transfers between devices: 72.3 us -> 0 us
  between operations: 14.7 us -> 0.74 us
  local copies, waits for them, and re-layouts: 16.7 us -> 7.46 us
  other arithmetic: 10.2 us -> 2.48 us
    psum x1 -> x0, waiting for transfers between devices: 213 us -> none  [body(): lax.psum(weight_term, ('frame', 'height', 'width')) / float(tile_count)]
    ppermute x24 -> x0, waiting for transfers between devices: 127 us -> none  [shifted(): return lax.ppermute(block, axis, route)]
    pallas_call x0 -> x2, Pallas kernels: none -> 72.9 us  [the longest x1 39.8 us: combine(): pl.pallas_call(combine_kernel, out_shape=(jax.ShapeDtypeStruct((2, ROWS,...]
    ppermute x24 -> x0, starting transfers between devices: 72.2 us -> none  [shifted(): return lax.ppermute(block, axis, route)]
    unnamed x31 -> x9, local copies, waits for them, and re-layouts: 8.99 us -> 2.43 us
    dot_general x20 -> x9, matrix products: 13.2 us -> 9.97 us  [the longest x1 1.6 us: body(): attended_grad = dot('tm,dm->td', grad_rows, out_weight).astype(bf16)]
  transfers between devices with their start and end apart: 25 -> 0, of which waited for: 13 -> 0; matrix products, arithmetic and copies ran while one was open for 4% -> 0% of each run, Pallas kernels for 0% -> 0%
where the time goes in v1:
time: 94.4 us; the launch traced here: 93.6 us
  Pallas kernels  72.9 us (77%)
  matrix products  9.97 us (11%)
  local copies, waits for them, and re-layouts  7.46 us (8%)
  other arithmetic  2.48 us (3%)
    pallas_call x1, Pallas kernels, combine(): pl.pallas_call(combine_kernel, out_shape=(jax.ShapeDtypeStruct((2, ROWS,...  39.8 us
    pallas_call x1, Pallas kernels, gather(): pl.pallas_call(gather_kernel, out_shape=jax.ShapeDtypeStruct((27, 2, ROWS...  33.1 us
    unnamed x9, local copies, waits for them, and re-layouts  2.43 us
    slice x1, local copies, waits for them, and re-layouts, body(): value_rows = window[:, 1].reshape(-1, DIM)  1.91 us

profile of v1, /device:TPU:1, one launch (start us, length us, event | category | flops | bytes accessed | tf_op | source)
XLA Modules:
  0.0 93.6 jit_solution(10966697155123886690)
XLA Ops:
  0.6 0.0 copy-start
  0.6 1.3 %copy-done = bf16[4,6,8,3072]{3,2,1,0:T(8,128)(2,1)S(1)} copy-done((bf16[4,6,8,3072]{3,2,1,0:T(8,128)(2,1)S(1)}, bf16[4,6,8,3072]{3,2,1,0:T(8,128)(2,1)}, u32[]{:S(2)}) %copy-start) | copy-done | bytes 1179672
  1.9 1.6 %convolution_convert_fusion.3 = bf16[192,128]{1,0:T(8,128)(2,1)S(1)} fusion(bf16[192,3072]{1,0:T(8,128)(2,1)S(1)} %bitcast.43, bf16[128,3072]{1,0:T(8,128)(2,1)} %param.8), kind=kOutput, calls=%fused_computation.16 | convolution fusion | flops 151019520 | bytes 2015232 | tf_op jit(solution)/shard_map/tm,dm->td/dot_general | solution.py:572
  3.5 33.1 %gather.1 = bf16[27,2,192,128]{3,2,1,0:T(8,128)(2,1)} custom-call(bf16[192,128]{1,0:T(8,128)(2,1)} %bitcast.58, bf16[192,128]{1,0:T(8,128)(2,1)} %bitcast.59), custom_call_target="tpu_custom_call" | custom-call | tf_op jit(solution)/shard_map/gather/pallas_call | solution.py:195
  36.6 0.0 copy-start.3
  36.6 1.9 %fusion.8 = (bf16[27,1,192,128]{3,2,1,0:T(8,128)(2,1)S(1)}, bf16[27,1,192,128]{3,2,1,0:T(8,128)(2,1)S(1)}) fusion(bf16[27,2,192,128]{3,2,1,0:T(8,128)(2,1)} %gather.1), kind=kLoop, calls=%fused_computation.19 | loop fusion | bytes 5308416 | tf_op jit(solution)/shard_map/slice | solution.py:562
  38.6 0.0 copy-done.3
  38.6 0.8 fusion.10
  39.4 0.7 fusion.4
  40.1 1.1 %multiply_reduce_fusion = (f32[192]{0:T(256)S(1)}, bf16[192,128]{1,0:T(8,128)(2,1)S(1)}) fusion(bf16[192,128]{1,0:T(8,128)(2,1)S(1)} %convolution_convert_fusion.3, bf16[5184,128]{1,0:T(8,128)(2,1)S(1)} %bitcast.50, f32[5184,192]{0,1:T(8,128)S(1)} %get-tuple-element.14, f32[192]{0:T(256)S(1)} %fusion.4, f32[192]{0:T(256)S(1)} %get-tuple-element.13), kind=kOutput, calls=%fused_computation.18 | convolution fusion | flops 256892736 | bytes 5409024 | tf_op jit(solution)/shard_map/qk,kd->qd/dot_general | solution.py:570
  41.2 1.2 %fusion.1 = bf16[192,5184]{1,0:T(8,128)(2,1)S(1)} fusion(bf16[192,128]{1,0:T(8,128)(2,1)S(1)} %convolution_convert_fusion.3, bf16[5184,128]{1,0:T(8,128)(2,1)S(1)} %bitcast.51, f32[192]{0:T(256)S(1)} %get-tuple-element.15, f32[192]{0:T(256)S(1)} %fusion.4, f32[5184,192]{0,1:T(8,128)S(1)} %get-tuple-element.14, f32[192]{0:T(256)S(1)} %get-tuple-element.13), kind=kOutput, calls=%fused_computation.3 | convolution fusion | flops 259780608 | bytes 7350528 | tf_op jit(solution)/shard_map/qd,kd->qk/dot_general | solution.py:575
  42.4 1.2 %fusion.12 = bf16[5184,128]{1,0:T(8,128)(2,1)S(1)} fusion(bf16[192,128]{1,0:T(8,128)(2,1)S(1)} %convolution_convert_fusion.3, f32[5184,192]{0,1:T(8,128)S(1)} %get-tuple-element.14, f32[192]{0:T(256)S(1)} %fusion.4, f32[192]{0:T(256)S(1)} %get-tuple-element.13), kind=kOutput, calls=%fused_computation.23 | convolution fusion | flops 256794624 | bytes 5359104 | tf_op jit(solution)/shard_map/qk,qd->kd/dot_general | solution.py:579
  43.5 1.3 %fusion.5 = bf16[192,128]{1,0:T(8,128)(2,1)} fusion(bf16[192,5184]{1,0:T(8,128)(2,1)S(1)} %fusion.1, bf16[5184,128]{1,0:T(8,128)(2,1)S(1)} %bitcast.46), kind=kOutput, calls=%fused_computation.15 | convolution fusion | flops 254853120 | bytes 3366912 | tf_op jit(solution)/shard_map/qk,kd->qd/dot_general | solution.py:577
  44.8 0.9 fusion.2
  45.8 1.8 %pad_maximum_fusion.parts = bf16[27,2,192,128]{3,2,1,0:T(8,128)(2,1)} fusion(bf16[27,1,192,128]{3,2,1,0:T(8,128)(2,1)S(1)} %bitcast.52, bf16[27,1,192,128]{3,2,1,0:T(8,128)(2,1)S(1)} %bitcast.47), kind=kLoop, calls=%fused_computation.13 | loop fusion | flops 1327104 | bytes 5308416 | tf_op jit(solution)/shard_map/stack | solution.py:580
  47.6 0.4 convolution_convert_fusion.2
  48.0 0.4 copy.11
  48.4 0.0 copy-start.1
  48.4 1.2 %copy.12 = bf16[2,12,128,128]{3,2,1,0:T(8,128)(2,1)} copy(bf16[2,12,128,128]{2,3,1,0:T(8,128)(2,1)S(1)} %bitcast.48) | data formatting | bytes 1572864 | tf_op jit(solution)/shard_map/transpose | solution.py:583
  49.5 39.8 %combine.1 = (bf16[2,192,128]{2,1,0:T(8,128)(2,1)}, f32[128,3072]{1,0:T(8,128)}) custom-call(bf16[27,2,192,128]{3,2,1,0:T(8,128)(2,1)} %pad_maximum_fusion.parts, bf16[2,1536,128]{2,1,0:T(8,128)(2,1)} %bitcast.49), custom_call_target="tpu_custom_call" | custom-call | tf_op jit(solution)/shard_map/combine/pallas_call | solution.py:510
  89.3 0.0 copy-start.2
  89.4 1.6 %fusion.9 = (bf16[1,192,128]{2,1,0:T(8,128)(2,1)}, bf16[1,192,128]{2,1,0:T(8,128)(2,1)}) fusion(bf16[2,192,128]{2,1,0:T(8,128)(2,1)} %get-tuple-element.7), kind=kLoop, calls=%fused_computation.20 | loop fusion | bytes 196608 | tf_op jit(solution)/shard_map/slice | solution.py:589
  90.9 0.0 copy-done.1
  90.9 1.5 %convolution_convert_fusion.1 = bf16[192,3072]{1,0:T(8,128)(2,1)} fusion(bf16[192,128]{1,0:T(8,128)(2,1)S(1)} %get-tuple-element.16, bf16[128,3072]{1,0:T(8,128)(2,1)S(1)} %copy-done.1), kind=kOutput, calls=%fused_computation.9 | convolution fusion | flops 151584768 | bytes 2015232 | tf_op jit(solution)/shard_map/qd,dm->qm/dot_general | solution.py:571
  92.4 0.0 copy-done.2
  92.4 1.1 %copy.14 = f32[128,3072]{1,0:T(8,128)} copy(f32[128,3072]{1,0:T(8,128)S(1)} %copy-done.2) | data formatting | bytes 3145728
Async XLA Ops:
  0.6 1.3 %copy-start = (bf16[4,6,8,3072]{3,2,1,0:T(8,128)(2,1)S(1)}, bf16[4,6,8,3072]{3,2,1,0:T(8,128)(2,1)}, u32[]{:S(2)}) copy-start(bf16[4,6,8,3072]{3,2,1,0:T(8,128)(2,1)} %param.9) | copy-start | bytes 3538948
  36.6 1.9 %copy-start.3 = (bf16[4,6,8,128]{3,2,1,0:T(8,128)(2,1)S(1)}, bf16[4,6,8,128]{3,2,1,0:T(8,128)(2,1)}, u32[]{:S(2)}) copy-start(bf16[4,6,8,128]{3,2,1,0:T(8,128)(2,1)} %param.5) | copy-start | bytes 147460
  48.4 42.6 %copy-start.1 = (bf16[128,3072]{1,0:T(8,128)(2,1)S(1)}, bf16[128,3072]{1,0:T(8,128)(2,1)}, u32[]{:S(2)}) copy-start(bf16[128,3072]{1,0:T(8,128)(2,1)} %param.8) | copy-start | bytes 2359300
  89.3 3.1 %copy-start.2 = (f32[128,3072]{1,0:T(8,128)S(1)}, f32[128,3072]{1,0:T(8,128)}, u32[]{:S(2)}) copy-start(f32[128,3072]{1,0:T(8,128)} %get-tuple-element.26) | copy-start | bytes 4718596

commit v2 on v1

v2 whole, which is shorter than its diff:
```python
import math

import jax
import jax.experimental.pallas as pl
import jax.experimental.pallas.tpu as pltpu
import jax.numpy as jnp
from jax import lax
from jax.sharding import PartitionSpec as P

MESH = pl.DeviceIdType.MESH
ROWS = 192
DIM = 128
LIMIT = 56 * 2**20
BF16, F32 = jnp.bfloat16, jnp.float32
ROOT = 1.0 / math.sqrt(DIM)
SCALE = ROOT * math.log2(math.e)


class Place:
    def __init__(self):
        self.f = lax.axis_index("frame")
        self.h = lax.axis_index("height")
        self.w = lax.axis_index("width")
        self.xlo = self.f // 2
        self.core = self.f - 2 * self.xlo
        self.xhi = self.w // 4
        self.y = self.w - 4 * self.xhi
        self.ring = (2 * self.xhi + self.xlo) * 4 + self.y
        self.sibling = (self.xlo * 2 + 1 - self.core, self.h, self.w)
        self.partner = ((1 - self.xlo) * 2 + self.core, self.h, self.w)
        self.own_plane = self.f - self.xlo
        self.sib_plane = self.xlo * 2 + 1 - self.core - self.xlo
        self.third_plane = 2 * (1 - self.xlo)
        self.collects = self.core == self.xlo
        self.supplies = self.core != self.xlo
        self.hslot = self.h - start(self.h)
        self.wslot = self.w - start(self.w)

    def plane_chip(self, index):
        x = index // 4
        y = index - 4 * x
        xhi = x // 2
        return ((x - 2 * xhi) * 2 + self.core, self.h, xhi * 4 + y)


def start(index):
    return jnp.maximum(jnp.minimum(index - 1, 5), 0)


def neighbours(index):
    return (
        (index >= 1, index - 1),
        (index <= 6, index + 1),
        ((index == 2) | (index == 5), 7 * (index // 5)),
    )


def owners(index):
    return (
        (index >= 1, index - 1),
        (index <= 6, index + 1),
        ((index == 0) | (index == 7), 2 + 3 * (index // 7)),
    )


def remote(src, dst, send_sem, recv_sem, target):
    return pltpu.make_async_remote_copy(
        src_ref=src,
        dst_ref=dst,
        send_sem=send_sem,
        recv_sem=recv_sem,
        device_id=target,
        device_id_type=MESH,
    )


def arrived(ref, sem):
    pltpu.make_async_copy(ref, ref, sem).wait()


def greet_plane(place, barrier):
    def one(k, carry):
        target = place.plane_chip(lax.rem(place.ring + k, 16))
        pl.semaphore_signal(barrier, inc=1, device_id=target, device_id_type=MESH)
        return carry

    lax.fori_loop(1, 16, one, 0)


def greet_column(place, barrier):
    def one(k, carry):
        target = (place.f, lax.rem(place.h + k, 8), place.w)
        pl.semaphore_signal(barrier, inc=1, device_id=target, device_id_type=MESH)
        return carry

    lax.fori_loop(1, 8, one, 0)


def greet_all(place):
    barrier = pltpu.get_barrier_semaphore()
    pl.semaphore_signal(barrier, inc=1, device_id=place.sibling, device_id_type=MESH)
    greet_plane(place, barrier)
    greet_column(place, barrier)
    pl.semaphore_wait(barrier, 23)


def begin(copies):
    for there, copy in copies:
        if there is True:
            copy.start()
        else:
            pl.when(there)(copy.start)


def finish(copies):
    for there, copy in copies:
        if there is True:
            copy.wait_send()
        else:
            pl.when(there)(copy.wait_send)


def tile_of(hslot):
    return pl.ds(pl.multiple_of(hslot * ROWS, ROWS), ROWS)


def piece_of(index):
    return pl.ds(pl.multiple_of(index * 96, 96), 96)


def dot(left, right, over):
    return lax.dot_general(left, right, ((over[:1], over[1:]), ((), ())), preferred_element_type=F32)


def kernel(
    q_ref, k_ref, v_ref, weight_hbm, grad_hbm,
    projected_hbm, query_out, kv_out, weight_out,
    kv, prob, prob_grad, col_max, run_max, run_sum, att, dquery, dout, dots,
    grads, weight, projected,
    terms, half, pieces, lines, full,
    parts, swap, third, cross, outgoing, wide, high,
    load_sem, store_sem,
    hsend, wsend, ssend, tsend, xsend, recv,
    half_sem, piece_send, piece_recv, line_send, line_recv, full_send, pass_send, full_recv,
    swap_send, swap_recv, third_send, third_recv, cross_send, cross_recv,
    wide_send, wide_recv, high_send, high_recv,
):
    place = Place()
    core, ring, h = place.core, place.ring, place.h
    own, sib, far = place.own_plane * 3, place.sib_plane * 3, place.third_plane * 3
    hslots = (place.hslot, lax.rem(place.hslot + 1, 3), lax.rem(place.hslot + 2, 3))
    wslots = (place.wslot, lax.rem(place.wslot + 1, 3), lax.rem(place.wslot + 2, 3))

    load_grads = pltpu.make_async_copy(grad_hbm, grads, load_sem.at[0])
    load_weight = pltpu.make_async_copy(weight_hbm, weight, load_sem.at[1])
    load_grads.start()
    load_weight.start()
    kv[own + place.wslot, 0, tile_of(place.hslot)] = k_ref[...]
    kv[own + place.wslot, 1, tile_of(place.hslot)] = v_ref[...]
    run_max[...] = jnp.full(run_max.shape, -jnp.inf, F32)
    run_sum[...] = jnp.zeros(run_sum.shape, F32)
    att[...] = jnp.zeros(att.shape, F32)
    dquery[...] = jnp.zeros(dquery.shape, F32)
    greet_all(place)

    def window(col, hslot):
        return kv.at[col, :, tile_of(hslot)]

    def along_height():
        col = own + place.wslot
        for i, (there, to) in enumerate(neighbours(h)):
            slot = h - start(to)
            yield there, remote(
                window(col, place.hslot), window(col, slot), hsend.at[i], recv.at[col, slot],
                (place.f, to, place.w),
            )

    def along_width(hslot):
        for i, (there, to) in enumerate(neighbours(place.w)):
            col = own + place.w - start(to)
            yield there, remote(
                window(own + place.wslot, hslot), window(col, hslot), wsend.at[i, hslot],
                recv.at[col, hslot], (place.f, h, to),
            )

    def along_frame(wslot, hslot):
        col = own + wslot
        to = 6 * place.xlo + wslot
        yield True, remote(
            window(col, hslot), window(col, hslot), ssend.at[wslot, hslot], recv.at[col, hslot],
            place.sibling,
        )
        yield place.supplies, remote(
            window(col, hslot), window(to, hslot), xsend.at[wslot, hslot], recv.at[to, hslot],
            place.partner,
        )

    def third_on(wslot, hslot):
        col = far + wslot
        yield place.collects, remote(
            window(col, hslot), window(col, hslot), tsend.at[wslot, hslot], recv.at[col, hslot],
            place.sibling,
        )

    def take(col, hslot):
        arrived(window(col, hslot), recv.at[col, hslot])

    def forward(col):
        keys, values = kv[col, 0], kv[col, 1]
        scores = dot(keys, q_ref[...], (1, 1))
        before = run_max[...]
        now = jnp.maximum(before, jnp.max(scores, axis=0, keepdims=True))
        shrink = jnp.exp2((before - now) * SCALE)
        weights = jnp.exp2((scores - now) * SCALE)
        run_max[...] = now
        col_max[col] = now
        run_sum[...] = run_sum[...] * shrink + jnp.sum(weights, axis=0, keepdims=True)
        prob[col] = weights
        att[...] = att[...] * shrink + dot(values, weights.astype(BF16), (0, 0))
        prob_grad[col] = dot(values, dout[...], (1, 1))

    begin(along_height())
    begin(along_width(hslots[0]))
    begin(along_frame(wslots[0], hslots[0]))
    load_grads.wait()
    load_weight.wait()
    dout[...] = dot(grads[...], weight[...], (1, 1)).astype(BF16)
    for hslot in hslots[1:]:
        take(own + wslots[0], hslot)
        begin(along_width(hslot))
        begin(along_frame(wslots[0], hslot))
    forward(own + wslots[0])
    for hslot in hslots[:2]:
        for wslot in wslots[1:]:
            take(own + wslot, hslot)
            begin(along_frame(wslot, hslot))
    for hslot in hslots:
        take(sib + wslots[0], hslot)
    forward(sib + wslots[0])
    for wslot in wslots[1:]:
        take(own + wslot, hslots[2])
        begin(along_frame(wslot, hslots[2]))
    for hslot in hslots:
        take(far + wslots[0], hslot)
        begin(third_on(wslots[0], hslot))
    forward(own + wslots[1])
    forward(far + wslots[0])
    for hslot in hslots[:2]:
        for wslot in wslots[1:]:
            take(far + wslot, hslot)
            begin(third_on(wslot, hslot))
    forward(own + wslots[2])
    for wslot in wslots[1:]:
        take(far + wslot, hslots[2])
        begin(third_on(wslot, hslots[2]))
    for wslot in wslots[1:]:
        for hslot in hslots:
            take(sib + wslot, hslot)
        forward(sib + wslot)
    for wslot in wslots[1:]:
        forward(far + wslot)

    inverse = 1.0 / run_sum[...]
    attended = (att[...] * inverse).astype(BF16)

    def weight_terms(side):
        def one(i, carry):
            columns = pl.ds(pl.multiple_of(side * 1536 + i * 512, 512), 512)
            term = dot(attended, grads[:, columns], (1, 0)).astype(BF16)
            for j in range(4):
                rows = pl.ds(pl.multiple_of(i * 512 + j * 128, 128), 128)
                terms[side, rows] = term[:, j * 128 : (j + 1) * 128]
            return carry

        lax.fori_loop(0, 3, one, 0)

    half_copy = remote(terms.at[1 - core], half, half_sem.at[0], half_sem.at[1], place.sibling)
    weight_terms(1 - core)
    half_copy.start()
    weight_terms(core)
    dots[...] = jnp.sum(
        jnp.transpose(dout[...].astype(F32)) * attended.astype(F32), axis=0, keepdims=True
    )

    def backward(col):
        share = jnp.exp2((col_max[col] - run_max[...]) * SCALE) / run_sum[...]
        probability = prob[col] * share
        score_grad = (probability * (prob_grad[col] - dots[...])).astype(BF16)
        parts[col, 1] = dot(probability.astype(BF16), dout[...], (1, 0)).astype(BF16)
        parts[col, 0] = (dot(score_grad, q_ref[...], (1, 0)) * ROOT).astype(BF16)
        dquery[...] += dot(kv[col, 0], score_grad, (0, 0))

    def swap_copy(wslot):
        return remote(
            parts.at[sib + wslot], swap.at[wslot], swap_send.at[wslot], swap_recv.at[wslot],
            place.sibling,
        )

    def third_copy(wslot):
        return remote(
            parts.at[far + wslot], third.at[wslot], third_send.at[wslot], third_recv.at[wslot],
            place.sibling,
        )

    def cross_copy(wslot, hslot):
        rows = tile_of(hslot)
        return remote(
            third.at[wslot, :, rows], cross.at[wslot, :, rows], cross_send.at[wslot, hslot],
            cross_recv.at[wslot, hslot], place.partner,
        )

    def third_column(wslot, carry):
        backward(far + wslot)
        pl.when(place.supplies)(third_copy(wslot).start)
        return carry

    lax.fori_loop(0, 3, third_column, 0)

    half_copy.wait()

    def add_half(piece, carry):
        rows = piece_of(piece)
        half[rows] = (terms[core, rows].astype(F32) + half[rows].astype(F32)).astype(BF16)
        return carry

    lax.fori_loop(0, 16, add_half, 0)

    def piece_copy(k):
        to = lax.rem(ring + k, 16)
        return remote(
            half.at[piece_of(to)], pieces.at[ring], piece_send.at[to], piece_recv.at[ring],
            place.plane_chip(to),
        )

    def start_piece(k, carry):
        piece_copy(k).start()
        return carry

    lax.fori_loop(1, 16, start_piece, 0)

    def sibling_column(wslot, carry):
        backward(sib + wslot)
        swap_copy(wslot).start()
        return carry

    lax.fori_loop(0, 3, sibling_column, 0)

    @pl.when(place.collects)
    def _():
        def one(wslot, carry):
            arrived(third.at[wslot], third_recv.at[wslot])
            for hslot in range(3):
                rows = tile_of(hslot)
                third[wslot, :, rows] = (
                    parts[far + wslot, :, rows].astype(F32) + third[wslot, :, rows].astype(F32)
                ).astype(BF16)
                cross_copy(wslot, hslot).start()
            return carry

        lax.fori_loop(0, 3, one, 0)

    def own_column(wslot, carry):
        backward(own + wslot)
        return carry

    lax.fori_loop(0, 3, own_column, 0)
    query_out[...] = (jnp.transpose(dquery[...]) * ROOT).astype(BF16)

    def project(i, carry):
        columns = pl.ds(pl.multiple_of(i * 512, 512), 512)
        projected[:, columns] = dot(attended, weight[:, columns], (0, 0)).astype(BF16)
        return carry

    lax.fori_loop(0, 6, project, 0)
    store = pltpu.make_async_copy(projected, projected_hbm, store_sem)
    store.start()

    mine = piece_of(ring)

    def add_piece(k, total):
        other = lax.rem(ring + k, 16)
        arrived(pieces.at[other], piece_recv.at[other])
        return total + pieces[other].astype(F32)

    total = lax.fori_loop(1, 16, add_piece, half[mine].astype(F32))
    lines[h] = total.astype(BF16)

    def line_copy(k):
        to = lax.rem(h + k, 8)
        return remote(
            lines.at[h], lines.at[h], line_send.at[to], line_recv.at[h], (place.f, to, place.w)
        )

    def start_line(k, carry):
        line_copy(k).start()
        return carry

    lax.fori_loop(1, 8, start_line, 0)

    def own_tile(wslot, hslot):
        rows = tile_of(hslot)
        outgoing[wslot, :, rows] = parts[own + wslot, :, rows].astype(F32) + swap[
            wslot, :, rows
        ].astype(F32)

        @pl.when(place.supplies)
        def _():
            arrived(cross.at[wslot, :, rows], cross_recv.at[wslot, hslot])
            outgoing[wslot, :, rows] += cross[wslot, :, rows].astype(F32)

        swap[wslot, :, rows] = outgoing[wslot, :, rows].astype(BF16)

    def width_copy(i, to, hslot):
        back = (1, 0, 2)[i]
        return remote(
            swap.at[to - start(place.w), :, tile_of(hslot)], wide.at[back, hslot],
            wide_send.at[i, hslot], wide_recv.at[back, hslot], (place.f, h, to),
        )

    for i, (there, to) in enumerate(owners(place.w)):

        @pl.when(there)
        def _():
            wslot = to - start(place.w)
            arrived(swap.at[wslot], swap_recv.at[wslot])

            def one(hslot, carry):
                own_tile(wslot, hslot)
                width_copy(i, to, hslot).start()
                return carry

            lax.fori_loop(0, 3, one, 0)

    def add_line(k, total):
        other = lax.rem(h + k, 8)
        arrived(lines.at[other], line_recv.at[other])
        return total + lines[other].astype(F32)

    total = lax.fori_loop(1, 8, add_line, total)
    full[core, mine] = (total * (1.0 / 256.0)).astype(BF16)

    def full_copy(k):
        to = lax.rem(ring + k, 16)
        return remote(
            full.at[core, mine], full.at[core, mine], full_send.at[to], full_recv.at[core, ring],
            place.plane_chip(to),
        )

    def pass_copy(piece):
        rows = piece_of(piece)
        return remote(
            full.at[core, rows], full.at[core, rows], pass_send.at[piece],
            full_recv.at[core, piece], place.sibling,
        )

    def start_full(k, carry):
        full_copy(k).start()
        return carry

    lax.fori_loop(1, 16, start_full, 0)
    pass_copy(ring).start()

    arrived(swap.at[place.wslot], swap_recv.at[place.wslot])

    def own_rows(hslot, carry):
        own_tile(place.wslot, hslot)
        return carry

    lax.fori_loop(0, 3, own_rows, 0)
    for i, (there, _w) in enumerate(neighbours(place.w)):

        @pl.when(there)
        def _():
            def one(hslot, carry):
                arrived(wide.at[i, hslot], wide_recv.at[i, hslot])
                outgoing[place.wslot, :, tile_of(hslot)] += wide[i, hslot].astype(F32)
                return carry

            lax.fori_loop(0, 3, one, 0)

    def height_copy(i, to):
        rows = tile_of(to - start(h))
        back = (1, 0, 2)[i]
        return remote(
            swap.at[place.wslot, :, rows], high.at[back], high_send.at[i], high_recv.at[back],
            (place.f, to, place.w),
        )

    for i, (there, to) in enumerate(owners(h)):

        @pl.when(there)
        def _():
            rows = tile_of(to - start(h))
            swap[place.wslot, :, rows] = outgoing[place.wslot, :, rows].astype(BF16)
            height_copy(i, to).start()

    def pass_on(k, carry):
        other = lax.rem(ring + k, 16)
        arrived(full.at[core, piece_of(other)], full_recv.at[core, other])
        pass_copy(other).start()
        return carry

    lax.fori_loop(1, 16, pass_on, 0)
    rows = tile_of(place.hslot)
    for i, (there, _h) in enumerate(neighbours(h)):

        @pl.when(there)
        def _():
            arrived(high.at[i], high_recv.at[i])
            outgoing[place.wslot, :, rows] += high[i].astype(F32)

    kv_out[...] = outgoing[place.wslot, :, rows].astype(BF16)

    def take_rest(piece, carry):
        arrived(full.at[1 - core, piece_of(piece)], full_recv.at[1 - core, piece])
        return carry

    lax.fori_loop(0, 16, take_rest, 0)
    for side in range(2):
        for block in range(12):
            weight_out[:, (side * 12 + block) * 128 : (side * 12 + block + 1) * 128] = full[
                side, block * 128 : (block + 1) * 128
            ].astype(F32)

    def left_plane(k, carry):
        piece_copy(k).wait_send()
        full_copy(k).wait_send()
        return carry

    lax.fori_loop(1, 16, left_plane, 0)

    def left_line(k, carry):
        line_copy(k).wait_send()
        return carry

    lax.fori_loop(1, 8, left_line, 0)

    def left_pass(piece, carry):
        pass_copy(piece).wait_send()
        return carry

    lax.fori_loop(0, 16, left_pass, 0)
    finish(along_height())

    def left_column(wslot, carry):
        swap_copy(wslot).wait_send()
        pl.when(place.supplies)(third_copy(wslot).wait_send)
        for hslot in range(3):
            finish(along_frame(wslot, hslot))
            finish(third_on(wslot, hslot))
            pl.when(place.collects)(cross_copy(wslot, hslot).wait_send)
        return carry

    lax.fori_loop(0, 3, left_column, 0)
    for hslot in range(3):
        finish(along_width(hslot))
    for i, (there, to) in enumerate(owners(place.w)):
        for hslot in range(3):
            pl.when(there)(width_copy(i, to, hslot).wait_send)
    for i, (there, to) in enumerate(owners(h)):
        pl.when(there)(height_copy(i, to).wait_send)
    store.wait()


def body(queries, key_vectors, value_vectors, out_weight, projected_grad):
    vmem, dma = pltpu.VMEM, pltpu.SemaphoreType.DMA
    model = out_weight.shape[1]
    column = (2, 3 * ROWS, DIM)
    here, there = pl.BlockSpec(memory_space=pltpu.VMEM), pl.BlockSpec(memory_space=pl.ANY)
    tile = (ROWS, DIM)
    projected, grad_query, kv_grad, grad_out_weight = pl.pallas_call(
        kernel,
        out_shape=(
            jax.ShapeDtypeStruct((ROWS, model), BF16),
            jax.ShapeDtypeStruct(tile, BF16),
            jax.ShapeDtypeStruct((2, ROWS, DIM), BF16),
            jax.ShapeDtypeStruct((DIM, model), F32),
        ),
        in_specs=[here, here, here, there, there],
        out_specs=[there, here, here, here],
        scratch_shapes=[
            vmem((9,) + column, BF16),
            vmem((9, 3 * ROWS, ROWS), F32),
            vmem((9, 3 * ROWS, ROWS), F32),
            vmem((9, 1, ROWS), F32),
            vmem((1, ROWS), F32),
            vmem((1, ROWS), F32),
            vmem((DIM, ROWS), F32),
            vmem((DIM, ROWS), F32),
            vmem(tile, BF16),
            vmem((1, ROWS), F32),
            vmem((ROWS, model), BF16),
            vmem((DIM, model), BF16),
            vmem((ROWS, model), BF16),
            vmem((2, 1536, DIM), BF16),
            vmem((1536, DIM), BF16),
            vmem((16, 96, DIM), BF16),
            vmem((8, 96, DIM), BF16),
            vmem((2, 1536, DIM), BF16),
            vmem((9,) + column, BF16),
            vmem((3,) + column, BF16),
            vmem((3,) + column, BF16),
            vmem((3,) + column, BF16),
            vmem((3,) + column, F32),
            vmem((3, 3, 2, ROWS, DIM), BF16),
            vmem((3, 2, ROWS, DIM), BF16),
            dma((2,)),
            dma,
            dma((3,)),
            dma((3, 3)),
            dma((3, 3)),
            dma((3, 3)),
            dma((3, 3)),
            dma((9, 3)),
            dma((2,)),
            dma((16,)),
            dma((16,)),
            dma((8,)),
            dma((8,)),
            dma((16,)),
            dma((16,)),
            dma((2, 16)),
            dma((3,)),
            dma((3,)),
            dma((3,)),
            dma((3,)),
            dma((3, 3)),
            dma((3, 3)),
            dma((3, 3)),
            dma((3, 3)),
            dma((3,)),
            dma((3,)),
        ],
        compiler_params=pltpu.CompilerParams(
            collective_id=0, has_side_effects=True, vmem_limit_bytes=LIMIT
        ),
        name="attention",
    )(
        queries.reshape(tile),
        key_vectors.reshape(tile),
        value_vectors.reshape(tile),
        out_weight,
        projected_grad.reshape(ROWS, model),
    )
    return (
        projected.reshape(projected_grad.shape),
        grad_query.reshape(queries.shape),
        kv_grad[0].reshape(queries.shape),
        kv_grad[1].reshape(queries.shape),
        grad_out_weight,
    )


def solution(mesh):
    spec = P("frame", "height", "width", None)
    return jax.shard_map(
        body,
        mesh=mesh,
        in_specs=(spec, spec, spec, P(), spec),
        out_specs=(spec, spec, spec, spec, P()),
        check_vma=False,
    )
```

time: 94.4 us -> 75.7 us (0.80)
  the two profiles are of different devices: /device:TPU:1 before, /device:TPU:16 now
where the time goes in v2:
time: 75.7 us; the launch traced here: 75.5 us
  Pallas kernels  69.1 us (91%)
  local copies, waits for them, and re-layouts  5.72 us (8%)
    pallas_call x1, Pallas kernels, body(): pl.pallas_call(kernel, out_shape=(jax.ShapeDtypeStruct((ROWS, model), BF1...  69.1 us
    unnamed x7, local copies, waits for them, and re-layouts  4.25 us

profile of v2, /device:TPU:16, one launch (start us, length us, event | category | flops | bytes accessed | tf_op | source)
XLA Modules:
  0.0 75.5 jit_solution(2294304310561079592)
XLA Ops:
  0.6 69.1 %attention.1 = (bf16[192,3072]{1,0:T(8,128)(2,1)}, bf16[192,128]{1,0:T(8,128)(2,1)}, bf16[2,192,128]{2,1,0:T(8,128)(2,1)}, f32[128,3072]{1,0:T(8,128)}) custom-call(bf16[192,128]{1,0:T(8,128)(2,1)} %bitcast.13, bf16[192,128]{1,0:T(8,128)(2,1)} %bitcast.14, bf16[192,128]{1,0:T(8,128)(2,1)} %bitcast.15, bf16[128,3072]{1,0:T(8,128)(2,1)} %weight_hbm.1, ...), custom_call_target="tpu_custom_call" | custom-call | tf_op jit(solution)/shard_map/attention/pallas_call | solution.py:571
  69.8 1.5 %fusion = (bf16[1,192,128]{2,1,0:T(8,128)(2,1)}, bf16[1,192,128]{2,1,0:T(8,128)(2,1)}) fusion(bf16[2,192,128]{2,1,0:T(8,128)(2,1)} %get-tuple-element.11), kind=kLoop, calls=%fused_computation | loop fusion | bytes 196608 | tf_op jit(solution)/shard_map/slice | solution.py:649
  71.2 0.0 copy-start.1
  71.2 0.0 copy-start
  71.2 2.5 %copy.13 = bf16[4,6,8,3072]{3,2,1,0:T(8,128)(2,1)} copy(bf16[4,6,8,3072]{3,2,1,0:T(8,128)(2,1)} %bitcast.8) | data formatting | bytes 2359296
  73.7 0.0 copy-done.1
  73.7 0.6 copy.14
  74.3 0.0 copy-done
  74.3 1.1 %copy.15 = f32[128,3072]{1,0:T(8,128)} copy(f32[128,3072]{1,0:T(8,128)S(1)} %copy-done) | data formatting | bytes 3145728
Async XLA Ops:
  71.2 2.5 %copy-start.1 = (bf16[192,128]{1,0:T(8,128)(2,1)S(1)}, bf16[192,128]{1,0:T(8,128)(2,1)}, u32[]{:S(2)}) copy-start(bf16[192,128]{1,0:T(8,128)(2,1)} %get-tuple-element.10) | copy-start | bytes 147460
  71.2 3.1 %copy-start = (f32[128,3072]{1,0:T(8,128)S(1)}, f32[128,3072]{1,0:T(8,128)}, u32[]{:S(2)}) copy-start(f32[128,3072]{1,0:T(8,128)} %get-tuple-element.24) | copy-start | bytes 4718596

commit v3 on v2

v3 whole, which is shorter than its diff:
```python
import math

import jax
import jax.experimental.pallas as pl
import jax.experimental.pallas.tpu as pltpu
import jax.numpy as jnp
from jax import lax
from jax.sharding import PartitionSpec as P

MESH = pl.DeviceIdType.MESH
ROWS = 192
WIDE = 256
DIM = 128
LIMIT = 56 * 2**20
BF16, F32 = jnp.bfloat16, jnp.float32
ROOT = 1.0 / math.sqrt(DIM)
SCALE = ROOT * math.log2(math.e)


class Place:
    def __init__(self):
        self.f = lax.axis_index("frame")
        self.h = lax.axis_index("height")
        self.w = lax.axis_index("width")
        self.xlo = self.f // 2
        self.core = self.f - 2 * self.xlo
        self.xhi = self.w // 4
        self.y = self.w - 4 * self.xhi
        self.ring = (2 * self.xhi + self.xlo) * 4 + self.y
        self.sibling = (self.xlo * 2 + 1 - self.core, self.h, self.w)
        self.partner = ((1 - self.xlo) * 2 + self.core, self.h, self.w)
        self.own_plane = self.core
        self.sib_plane = 1 - self.core
        self.lent_plane = 1 - self.xlo
        self.lends_own = self.core != self.xlo
        self.lends_sib = self.core == self.xlo
        self.hslot = self.h - start(self.h)
        self.wslot = self.w - start(self.w)

    def plane_chip(self, index):
        x = index // 4
        y = index - 4 * x
        xhi = x // 2
        return ((x - 2 * xhi) * 2 + self.core, self.h, xhi * 4 + y)

    def plane_shift(self, k):
        x = lax.rem(2 * self.xhi + self.xlo + k // 4, 4)
        return x * 4 + lax.rem(self.y + lax.rem(k, 4), 4)


def start(index):
    return jnp.maximum(jnp.minimum(index - 1, 5), 0)


def neighbours(index):
    return (
        (index >= 1, index - 1),
        (index <= 6, index + 1),
        ((index == 2) | (index == 5), 7 * (index // 5)),
    )


def owners(index):
    return (
        (index >= 1, index - 1),
        (index <= 6, index + 1),
        ((index == 0) | (index == 7), 2 + 3 * (index // 7)),
    )


def remote(src, dst, send_sem, recv_sem, target):
    return pltpu.make_async_remote_copy(
        src_ref=src,
        dst_ref=dst,
        send_sem=send_sem,
        recv_sem=recv_sem,
        device_id=target,
        device_id_type=MESH,
    )


def arrived(ref, sem):
    pltpu.make_async_copy(ref, ref, sem).wait()


def greet_all(place):
    barrier = pltpu.get_barrier_semaphore()

    def greet(target):
        pl.semaphore_signal(barrier, inc=1, device_id=target, device_id_type=MESH)

    for k in (4, 3, 5, 2, 6):
        greet((place.f, lax.rem(place.h + k, 8), place.w))
    for k in (10, 6, 9, 11, 14, 2, 5, 7, 8, 13, 15, 1, 3, 4, 12):
        greet(place.plane_chip(place.plane_shift(k)))
    for k in (1, 7):
        greet((place.f, lax.rem(place.h + k, 8), place.w))
    greet(place.sibling)


def begin(copies):
    for there, copy in copies:
        if there is True:
            copy.start()
        else:
            pl.when(there)(copy.start)


def finish(copies):
    for there, copy in copies:
        if there is True:
            copy.wait_send()
        else:
            pl.when(there)(copy.wait_send)


def tile_of(hslot):
    return pl.ds(pl.multiple_of(hslot * ROWS, ROWS), ROWS)


def piece_of(index, chunk):
    return pl.ds(pl.multiple_of(index * 96 + chunk * 48, 48), 48)


def far_first(i):
    return 1 + lax.rem(i + 9, 15)


def dot(left, right, over):
    return lax.dot_general(left, right, ((over[:1], over[1:]), ((), ())), preferred_element_type=F32)


def kernel(
    q_ref, k_ref, v_ref, weight_hbm, grad_hbm,
    projected_hbm, query_out, kv_out, full,
    kv, queries, douts, own_prob, own_grad, own_max, lent_prob, lent_grad, lent_max,
    own_state, lent_state, own_att, lent_att, att_out, att_in, state_out, state_in,
    stats_out, stats_in, dquery, dquery_out, dquery_in,
    grads, weight, projected,
    terms, half, pieces, lines,
    parts, swap, outgoing, wide, tall, high, side,
    load_sem, store_sem,
    hsend, wsend, ssend, recv, xsend, xrecv,
    half_sem, piece_send, piece_recv, line_send, line_recv, full_send, pass_send, full_recv,
    swap_send, swap_recv, wide_send, wide_recv, tall_send, tall_recv,
    high_send, high_recv, side_send, side_recv,
):
    place = Place()
    core, ring, h = place.core, place.ring, place.h
    own, sib, lent = place.own_plane * 3, place.sib_plane * 3, place.lent_plane * 3
    kept = 3 - lent
    hslots = (place.hslot, lax.rem(place.hslot + 1, 3), lax.rem(place.hslot + 2, 3))
    wslots = (place.wslot, lax.rem(place.wslot + 1, 3), lax.rem(place.wslot + 2, 3))
    mine, theirs = pl.ds(0, ROWS), pl.ds(WIDE, ROWS)

    greet_all(place)
    load_grads = pltpu.make_async_copy(grad_hbm, grads, load_sem.at[0])
    load_weight = pltpu.make_async_copy(weight_hbm, weight, load_sem.at[1])
    load_grads.start()
    load_weight.start()
    kv[own + place.wslot, 0, tile_of(place.hslot)] = k_ref[...]
    kv[own + place.wslot, 1, tile_of(place.hslot)] = v_ref[...]
    queries[mine] = q_ref[...]
    for first in (ROWS, WIDE + ROWS):
        queries[first : first + WIDE - ROWS] = jnp.zeros((WIDE - ROWS, DIM), BF16)
        douts[first : first + WIDE - ROWS] = jnp.zeros((WIDE - ROWS, DIM), BF16)
    for state, total in ((own_state, own_att), (lent_state, lent_att)):
        state[...] = jnp.zeros(state.shape, F32)
        state[0:1] = jnp.full((1, state.shape[1]), -jnp.inf, F32)
        total[...] = jnp.zeros(total.shape, F32)
    stats_out[...] = jnp.zeros(stats_out.shape, F32)
    dquery[...] = jnp.zeros(dquery.shape, F32)
    load_grads.wait()
    load_weight.wait()
    douts[mine] = dot(grads[...], weight[...], (1, 1)).astype(BF16)
    pl.semaphore_wait(pltpu.get_barrier_semaphore(), 23)

    def over(i, source, target):
        return remote(source, target, xsend.at[i], xrecv.at[i], place.partner)

    query_copy = over(0, queries.at[mine], queries.at[theirs])
    dout_copy = over(1, douts.at[mine], douts.at[theirs])
    att_copy = over(2, att_out, att_in)
    state_copy = over(3, state_out, state_in)
    stats_copy = over(4, stats_out, stats_in)
    dquery_copy = over(5, dquery_out, dquery_in)

    def window(col, hslot, part):
        return kv.at[col, part, tile_of(hslot)]

    def along_height(wslot, part):
        col = own + wslot
        for i, (there, to) in enumerate(neighbours(h)):
            slot = h - start(to)
            yield there, remote(
                window(col, place.hslot, part), window(col, slot, part),
                hsend.at[i, wslot, part], recv.at[col, slot, part], (place.f, to, place.w),
            )

    def along_width(hslot, part):
        for i, (there, to) in enumerate(neighbours(place.w)):
            col = own + place.w - start(to)
            yield there, remote(
                window(own + place.wslot, hslot, part), window(col, hslot, part),
                wsend.at[i, hslot, part], recv.at[col, hslot, part], (place.f, h, to),
            )

    def to_sibling(wslot, hslot, part):
        col = own + wslot
        yield True, remote(
            window(col, hslot, part), window(col, hslot, part), ssend.at[wslot, hslot, part],
            recv.at[col, hslot, part], place.sibling,
        )

    def take(plane, wslot, hslot, part):
        col = plane + wslot
        arrived(window(col, hslot, part), recv.at[col, hslot, part])

    def forward(plane, tiles, prob, prob_grad, col_max, state, total):
        width = state.shape[1]
        rows = [tile_of(hslot) for _, hslot in tiles]
        scores = [
            dot(kv[plane + wslot, 0, row], queries[:width], (1, 1))
            for (wslot, _), row in zip(tiles, rows)
        ]
        before = state[0:1]
        now = before
        for score in scores:
            now = jnp.maximum(now, jnp.max(score, axis=0, keepdims=True))
        shrink = jnp.exp2((before - now) * SCALE)
        row_sum = state[1:2] * shrink
        added = jnp.zeros((DIM, width), F32)
        for (wslot, hslot), row, score in zip(tiles, rows, scores):
            weights = jnp.exp2((score - now) * SCALE)
            row_sum += jnp.sum(weights, axis=0, keepdims=True)
            values = kv[plane + wslot, 1, row]
            prob[wslot, row] = weights
            prob_grad[wslot, row] = dot(values, douts[:width], (1, 1))
            col_max[wslot, hslot] = now
            added += dot(values, weights.astype(BF16), (0, 0))
        state[0:1] = now
        state[1:2] = row_sum
        total[...] = total[...] * shrink + added

    def forward_own(tiles):
        forward(kept, tiles, own_prob, own_grad, own_max, own_state, own_att)

    def forward_lent(tiles):
        forward(lent, tiles, lent_prob, lent_grad, lent_max, lent_state, lent_att)

    w0, h0 = wslots[0], hslots[0]
    begin(along_height(w0, 0))
    begin(along_width(h0, 1))
    begin(along_width(h0, 0))
    begin(along_height(w0, 1))
    begin(to_sibling(w0, h0, 0))
    begin(to_sibling(w0, h0, 1))
    query_copy.start()
    dout_copy.start()
    for wslot, hslot in zip(wslots[1:], hslots[1:]):
        take(own, w0, hslot, 0)
        begin(along_width(hslot, 0))
        begin(to_sibling(w0, hslot, 0))
        take(own, wslot, h0, 1)
        begin(along_height(wslot, 1))
        begin(to_sibling(wslot, h0, 1))
    for wslot, hslot in zip(wslots[1:], hslots[1:]):
        take(own, w0, hslot, 1)
        begin(to_sibling(w0, hslot, 1))
        take(own, wslot, h0, 0)
        begin(to_sibling(wslot, h0, 0))
    query_copy.wait()
    dout_copy.wait()
    steps = [[(w0, hslot) for hslot in hslots]]
    steps += [[(wslot, hslot) for wslot in wslots[1:]] for hslot in hslots]

    def from_corners(tiles):
        for part in range(2):
            for wslot, hslot in tiles:
                take(own, wslot, hslot, part)
                begin(to_sibling(wslot, hslot, part))

    for i in range(4):
        for wslot, hslot in steps[i]:
            for part in range(2):
                take(sib, wslot, hslot, part)
        if i < 3:
            forward_lent(steps[i])
            forward_own(steps[i])
        if 0 < i < 3:
            from_corners(steps[i + 1])
    forward_lent(steps[3])
    att_out[...] = lent_att[:, WIDE:].astype(BF16)
    state_out[...] = lent_state[:, WIDE:]
    att_copy.start()
    state_copy.start()
    forward_own(steps[3])

    att_copy.wait()
    state_copy.wait()
    shares = [
        (own_state[...], own_att[...]),
        (lent_state[:, :WIDE], lent_att[:, :WIDE]),
        (state_in[...], att_in[...].astype(F32)),
    ]
    row_max = jnp.maximum(jnp.maximum(shares[0][0][0:1], shares[1][0][0:1]), shares[2][0][0:1])
    row_sum = jnp.zeros((1, WIDE), F32)
    total = jnp.zeros((DIM, WIDE), F32)
    for state, partial in shares:
        shrink = jnp.exp2((state[0:1] - row_max) * SCALE)
        row_sum += state[1:2] * shrink
        total += partial * shrink
    inverse = 1.0 / row_sum
    attended_wide = (total * inverse).astype(BF16)
    attended = attended_wide[:, :ROWS]

    def weight_terms(side):
        def one(i, carry):
            columns = pl.ds(pl.multiple_of(side * 1536 + i * 512, 512), 512)
            term = dot(attended, grads[:, columns], (1, 0)).astype(BF16)
            for j in range(4):
                rows = pl.ds(pl.multiple_of(i * 512 + j * 128, 128), 128)
                terms[side, rows] = term[:, j * 128 : (j + 1) * 128]
            return carry

        lax.fori_loop(0, 3, one, 0)

    half_copy = remote(terms.at[1 - core], half, half_sem.at[0], half_sem.at[1], place.sibling)
    weight_terms(1 - core)
    half_copy.start()
    stats_out[0:1] = row_max
    stats_out[1:2] = inverse
    stats_out[2:3] = jnp.sum(
        jnp.transpose(douts[:WIDE].astype(F32)) * attended_wide.astype(F32), axis=0, keepdims=True
    )
    stats_copy.start()
    weight_terms(core)

    def backward(plane, wslot, prob, prob_grad, col_max, stats):
        width = prob.shape[2]
        added = jnp.zeros((DIM, width), F32)
        for hslot in range(3):
            rows = tile_of(hslot)
            share = jnp.exp2((col_max[wslot, hslot] - stats[0]) * SCALE) * stats[1]
            probability = prob[wslot, rows] * share
            score_grad = (probability * (prob_grad[wslot, rows] - stats[2])).astype(BF16)
            value_part = dot(probability.astype(BF16), douts[:width], (1, 0))
            key_part = dot(score_grad, queries[:width], (1, 0)) * ROOT
            parts[plane + wslot, 1, rows] = value_part.astype(BF16)
            parts[plane + wslot, 0, rows] = key_part.astype(BF16)
            added += dot(kv[plane + wslot, 0, rows], score_grad, (0, 0))
        dquery[:, :width] += added

    def swap_copy(wslot):
        return remote(
            parts.at[sib + wslot], swap.at[wslot], swap_send.at[wslot], swap_recv.at[wslot],
            place.sibling,
        )

    def own_column(wslot, carry):
        stats = [stats_out[i : i + 1] for i in range(3)]
        backward(kept, wslot, own_prob, own_grad, own_max, stats)
        pl.when(place.lends_own)(swap_copy(wslot).start)
        return carry

    lax.fori_loop(0, 3, own_column, 0)

    half_copy.wait()

    def piece_copy(chunk, k):
        to = place.plane_shift(k)
        return remote(
            half.at[piece_of(to, chunk)], pieces.at[chunk, ring], piece_send.at[chunk, to],
            piece_recv.at[chunk, ring], place.plane_chip(to),
        )

    def scatter(chunk):
        def add_half(piece, carry):
            rows = piece_of(piece, chunk)
            half[rows] = (terms[core, rows].astype(F32) + half[rows].astype(F32)).astype(BF16)
            return carry

        def start_piece(i, carry):
            piece_copy(chunk, far_first(i)).start()
            return carry

        lax.fori_loop(0, 16, add_half, 0)
        lax.fori_loop(0, 15, start_piece, 0)

    scatter(0)
    scatter(1)
    stats_copy.wait()

    def lent_column(wslot, carry):
        stats = [
            jnp.concatenate([stats_out[i : i + 1], stats_in[i : i + 1]], axis=1) for i in range(3)
        ]
        backward(lent, wslot, lent_prob, lent_grad, lent_max, stats)
        pl.when(place.lends_sib)(swap_copy(wslot).start)
        return carry

    lax.fori_loop(0, 3, lent_column, 0)
    dquery_out[...] = dquery[:, WIDE:]
    dquery_copy.start()

    def own_tile(wslot, hslot):
        rows = tile_of(hslot)
        outgoing[wslot, :, rows] = parts[own + wslot, :, rows].astype(F32) + swap[
            wslot, :, rows
        ].astype(F32)
        swap[wslot, :, rows] = outgoing[wslot, :, rows].astype(BF16)

    back = (1, 0, 2)

    def width_copy(i, to, hslot):
        return remote(
            swap.at[to - start(place.w), 0, tile_of(hslot)], wide.at[back[i], hslot],
            wide_send.at[i, hslot], wide_recv.at[back[i], hslot], (place.f, h, to),
        )

    def tall_copy(i, to, wslot):
        return remote(
            swap.at[wslot, 1, tile_of(to - start(h))], tall.at[back[i], wslot],
            tall_send.at[i, wslot], tall_recv.at[back[i], wslot], (place.f, to, place.w),
        )

    def own_rows(wslot, carry):
        arrived(swap.at[wslot], swap_recv.at[wslot])
        for hslot in range(3):
            own_tile(wslot, hslot)
        return carry

    lax.fori_loop(0, 3, own_rows, 0)

    def three(body):
        def one(slot, carry):
            body(slot)
            return carry

        lax.fori_loop(0, 3, one, 0)

    for i, (there, to) in enumerate(owners(place.w)):
        pl.when(there)(lambda: three(lambda slot: width_copy(i, to, slot).start()))
    for i, (there, to) in enumerate(owners(h)):
        pl.when(there)(lambda: three(lambda slot: tall_copy(i, to, slot).start()))

    def project(i, carry):
        columns = pl.ds(pl.multiple_of(i * 512, 512), 512)
        projected[:, columns] = dot(attended, weight[:, columns], (0, 0)).astype(BF16)
        return carry

    lax.fori_loop(0, 6, project, 0)
    store = pltpu.make_async_copy(projected, projected_hbm, store_sem)
    store.start()
    dquery_copy.wait()
    query_out[...] = (jnp.transpose(dquery[:, :WIDE] + dquery_in[...])[:ROWS] * ROOT).astype(BF16)

    def line_copy(chunk, k):
        to = lax.rem(h + k, 8)
        return remote(
            lines.at[chunk, h], lines.at[chunk, h], line_send.at[chunk, to],
            line_recv.at[chunk, h], (place.f, to, place.w),
        )

    def exchange(chunk):
        def add_piece(k, total):
            other = place.plane_shift(k)
            arrived(pieces.at[chunk, other], piece_recv.at[chunk, other])
            return total + pieces[chunk, other].astype(F32)

        def start_line(k, carry):
            line_copy(chunk, k).start()
            return carry

        total = lax.fori_loop(1, 16, add_piece, half[piece_of(ring, chunk)].astype(F32))
        lines[chunk, h] = total.astype(BF16)
        lax.fori_loop(1, 8, start_line, 0)
        return total

    totals = [exchange(0), exchange(1)]

    def add_wide(i, hslot):
        arrived(wide.at[i, hslot], wide_recv.at[i, hslot])
        outgoing[place.wslot, 0, tile_of(hslot)] += wide[i, hslot].astype(F32)

    def add_tall(i, wslot):
        arrived(tall.at[i, wslot], tall_recv.at[i, wslot])
        outgoing[wslot, 1, tile_of(place.hslot)] += tall[i, wslot].astype(F32)

    for i, (there, _w) in enumerate(neighbours(place.w)):
        pl.when(there)(lambda: three(lambda slot: add_wide(i, slot)))
    for i, (there, _h) in enumerate(neighbours(h)):
        pl.when(there)(lambda: three(lambda slot: add_tall(i, slot)))

    def height_copy(i, to):
        rows = tile_of(to - start(h))
        return remote(
            swap.at[place.wslot, 0, rows], high.at[back[i]], high_send.at[i],
            high_recv.at[back[i]], (place.f, to, place.w),
        )

    def side_copy(i, to):
        rows = tile_of(place.hslot)
        return remote(
            swap.at[to - start(place.w), 1, rows], side.at[back[i]], side_send.at[i],
            side_recv.at[back[i]], (place.f, h, to),
        )

    for i, (there, to) in enumerate(owners(h)):

        @pl.when(there)
        def _():
            rows = tile_of(to - start(h))
            swap[place.wslot, 0, rows] = outgoing[place.wslot, 0, rows].astype(BF16)
            height_copy(i, to).start()

    for i, (there, to) in enumerate(owners(place.w)):

        @pl.when(there)
        def _():
            rows = tile_of(place.hslot)
            wslot = to - start(place.w)
            swap[wslot, 1, rows] = outgoing[wslot, 1, rows].astype(BF16)
            side_copy(i, to).start()

    def full_copy(chunk, k):
        to = place.plane_shift(k)
        rows = piece_of(ring, chunk)
        return remote(
            full.at[core, rows], full.at[core, rows], full_send.at[chunk, to],
            full_recv.at[core, chunk, ring], place.plane_chip(to),
        )

    def pass_copy(chunk, piece):
        rows = piece_of(piece, chunk)
        return remote(
            full.at[core, rows], full.at[core, rows], pass_send.at[chunk, piece],
            full_recv.at[core, chunk, piece], place.sibling,
        )

    def spread(chunk):
        def add_line(k, total):
            other = lax.rem(h + k, 8)
            arrived(lines.at[chunk, other], line_recv.at[chunk, other])
            return total + lines[chunk, other].astype(F32)

        def start_full(i, carry):
            full_copy(chunk, far_first(i)).start()
            return carry

        total = lax.fori_loop(1, 8, add_line, totals[chunk])
        full[core, piece_of(ring, chunk)] = (total * (1.0 / 256.0)).astype(BF16)
        lax.fori_loop(0, 15, start_full, 0)
        pass_copy(chunk, ring).start()

    spread(0)
    spread(1)

    rows = tile_of(place.hslot)
    for i, (there, _h) in enumerate(neighbours(h)):

        @pl.when(there)
        def _():
            arrived(high.at[i], high_recv.at[i])
            outgoing[place.wslot, 0, rows] += high[i].astype(F32)

    for i, (there, _w) in enumerate(neighbours(place.w)):

        @pl.when(there)
        def _():
            arrived(side.at[i], side_recv.at[i])
            outgoing[place.wslot, 1, rows] += side[i].astype(F32)

    kv_out[...] = outgoing[place.wslot, :, rows].astype(BF16)

    for chunk in range(2):

        def pass_on(k, carry):
            other = place.plane_shift(k)
            arrived(full.at[core, piece_of(other, chunk)], full_recv.at[core, chunk, other])
            pass_copy(chunk, other).start()
            return carry

        lax.fori_loop(1, 16, pass_on, 0)

    def take_rest(piece, carry):
        for chunk in range(2):
            arrived(
                full.at[1 - core, piece_of(piece, chunk)], full_recv.at[1 - core, chunk, piece]
            )
        return carry

    lax.fori_loop(0, 16, take_rest, 0)

    def left_plane(k, carry):
        for chunk in range(2):
            piece_copy(chunk, k).wait_send()
            full_copy(chunk, k).wait_send()
        return carry

    lax.fori_loop(1, 16, left_plane, 0)

    def left_line(k, carry):
        for chunk in range(2):
            line_copy(chunk, k).wait_send()
        return carry

    lax.fori_loop(1, 8, left_line, 0)

    def left_pass(piece, carry):
        for chunk in range(2):
            pass_copy(chunk, piece).wait_send()
        return carry

    lax.fori_loop(0, 16, left_pass, 0)
    def left_column(slot, carry):
        swap_copy(slot).wait_send()
        for hslot in range(3):
            for part in range(2):
                finish(to_sibling(slot, hslot, part))
        finish(along_width(slot, 0))
        finish(along_height(slot, 1))
        return carry

    lax.fori_loop(0, 3, left_column, 0)
    finish(along_height(w0, 0))
    finish(along_width(h0, 1))
    for i, (there, to) in enumerate(owners(place.w)):
        pl.when(there)(lambda: three(lambda slot: width_copy(i, to, slot).wait_send()))
        pl.when(there)(side_copy(i, to).wait_send)
    for i, (there, to) in enumerate(owners(h)):
        pl.when(there)(lambda: three(lambda slot: tall_copy(i, to, slot).wait_send()))
        pl.when(there)(height_copy(i, to).wait_send)
    store.wait()


def write_kernel(
    projected, query, kv, full, projected_out, query_out, key_out, value_out, weight_out,
    rows, tiles, held, wide, load_sem, store_sem,
):
    pairs = [
        (full.at[0], held.at[0], None),
        (full.at[1], held.at[1], None),
        (query, tiles.at[0], query_out),
        (kv.at[0], tiles.at[1], key_out),
        (kv.at[1], tiles.at[2], value_out),
    ]
    for i in range(4):
        part = pl.ds(i * 48, 48)
        pairs.append((projected.at[part], rows.at[part], projected_out.at[part]))
    loads = [
        pltpu.make_async_copy(source, here, load_sem.at[i])
        for i, (source, here, _) in enumerate(pairs)
    ]
    for load in loads:
        load.start()
    stores = []
    for i, (_, here, target) in enumerate(pairs):
        loads[i].wait()
        if i < 2:
            for block in range(12):
                wide[i, :, block * 128 : (block + 1) * 128] = held[
                    i, block * 128 : (block + 1) * 128
                ].astype(F32)
            here, target = wide.at[i], weight_out.at[:, i * 1536 : (i + 1) * 1536]
        stores.append(pltpu.make_async_copy(here, target, store_sem.at[i]))
        stores[i].start()
    for store in stores:
        store.wait()


def body(queries, key_vectors, value_vectors, out_weight, projected_grad):
    vmem, dma = pltpu.VMEM, pltpu.SemaphoreType.DMA
    model = out_weight.shape[1]
    column = (2, 3 * ROWS, DIM)
    here, there = pl.BlockSpec(memory_space=pltpu.VMEM), pl.BlockSpec(memory_space=pl.ANY)
    tile = (ROWS, DIM)
    results = pl.pallas_call(
        kernel,
        out_shape=(
            jax.ShapeDtypeStruct((ROWS, model), BF16),
            jax.ShapeDtypeStruct(tile, BF16),
            jax.ShapeDtypeStruct((2, ROWS, DIM), BF16),
            jax.ShapeDtypeStruct((2, 1536, DIM), BF16),
        ),
        in_specs=[here, here, here, there, there],
        out_specs=[there, here, here, here],
        scratch_shapes=[
            vmem((6,) + column, BF16),
            vmem((2 * WIDE, DIM), BF16),
            vmem((2 * WIDE, DIM), BF16),
            vmem((3, 3 * ROWS, WIDE), F32),
            vmem((3, 3 * ROWS, WIDE), F32),
            vmem((3, 3, 1, WIDE), F32),
            vmem((3, 3 * ROWS, 2 * WIDE), F32),
            vmem((3, 3 * ROWS, 2 * WIDE), F32),
            vmem((3, 3, 1, 2 * WIDE), F32),
            vmem((8, WIDE), F32),
            vmem((8, 2 * WIDE), F32),
            vmem((DIM, WIDE), F32),
            vmem((DIM, 2 * WIDE), F32),
            vmem((DIM, WIDE), BF16),
            vmem((DIM, WIDE), BF16),
            vmem((8, WIDE), F32),
            vmem((8, WIDE), F32),
            vmem((8, WIDE), F32),
            vmem((8, WIDE), F32),
            vmem((DIM, 2 * WIDE), F32),
            vmem((DIM, WIDE), F32),
            vmem((DIM, WIDE), F32),
            vmem((ROWS, model), BF16),
            vmem((DIM, model), BF16),
            vmem((ROWS, model), BF16),
            vmem((2, 1536, DIM), BF16),
            vmem((1536, DIM), BF16),
            vmem((2, 16, 48, DIM), BF16),
            vmem((2, 8, 48, DIM), BF16),
            vmem((6,) + column, BF16),
            vmem((3,) + column, BF16),
            vmem((3,) + column, F32),
            vmem((3, 3) + tile, BF16),
            vmem((3, 3) + tile, BF16),
            vmem((3,) + tile, BF16),
            vmem((3,) + tile, BF16),
            dma((2,)),
            dma,
            dma((3, 3, 2)),
            dma((3, 3, 2)),
            dma((3, 3, 2)),
            dma((6, 3, 2)),
            dma((6,)),
            dma((6,)),
            dma((2,)),
            dma((2, 16)),
            dma((2, 16)),
            dma((2, 8)),
            dma((2, 8)),
            dma((2, 16)),
            dma((2, 16)),
            dma((2, 2, 16)),
            dma((3,)),
            dma((3,)),
            dma((3, 3)),
            dma((3, 3)),
            dma((3, 3)),
            dma((3, 3)),
            dma((3,)),
            dma((3,)),
            dma((3,)),
            dma((3,)),
        ],
        compiler_params=pltpu.CompilerParams(
            collective_id=0, has_side_effects=True, vmem_limit_bytes=LIMIT
        ),
        name="attention",
    )(
        queries.reshape(tile),
        key_vectors.reshape(tile),
        value_vectors.reshape(tile),
        out_weight,
        projected_grad.reshape(ROWS, model),
    )
    projected, grad_query, grad_key, grad_value, grad_out_weight = pl.pallas_call(
        write_kernel,
        out_shape=(
            jax.ShapeDtypeStruct((ROWS, model), BF16),
            jax.ShapeDtypeStruct(tile, BF16),
            jax.ShapeDtypeStruct(tile, BF16),
            jax.ShapeDtypeStruct(tile, BF16),
            jax.ShapeDtypeStruct((DIM, model), F32),
        ),
        in_specs=[there] * 4,
        out_specs=[there] * 5,
        scratch_shapes=[
            vmem((ROWS, model), BF16),
            vmem((3,) + tile, BF16),
            vmem((2, 1536, DIM), BF16),
            vmem((2, DIM, 1536), F32),
            dma((9,)),
            dma((9,)),
        ],
        compiler_params=pltpu.CompilerParams(vmem_limit_bytes=LIMIT),
        name="write",
    )(*results)
    return (
        projected.reshape(projected_grad.shape),
        grad_query.reshape(queries.shape),
        grad_key.reshape(queries.shape),
        grad_value.reshape(queries.shape),
        grad_out_weight,
    )


def solution(mesh):
    spec = P("frame", "height", "width", None)
    return jax.shard_map(
        body,
        mesh=mesh,
        in_specs=(spec, spec, spec, P(), spec),
        out_specs=(spec, spec, spec, spec, P()),
        check_vma=False,
    )
```

time: 75.7 us -> 64.6 us (0.85)
  the two profiles are of different devices: /device:TPU:16 before, /device:TPU:1 now
where the time goes in v3:
time: 64.6 us; the launch traced here: 64.4 us
  Pallas kernels  63.7 us (99%)
    pallas_call x1, Pallas kernels, body(): pl.pallas_call(kernel, out_shape=(jax.ShapeDtypeStruct((ROWS, model), BF1...  60.9 us
    pallas_call x1, Pallas kernels, body(): pl.pallas_call(write_kernel, out_shape=(jax.ShapeDtypeStruct((ROWS, model...  2.8 us

profile of v3, /device:TPU:1, one launch (start us, length us, event | category | flops | bytes accessed | tf_op | source)
XLA Modules:
  0.0 64.4 jit_solution(7260562330543152633)
XLA Ops:
  0.6 60.9 %attention.1 = (bf16[192,3072]{1,0:T(8,128)(2,1)}, bf16[192,128]{1,0:T(8,128)(2,1)}, bf16[2,192,128]{2,1,0:T(8,128)(2,1)}, bf16[2,1536,128]{2,1,0:T(8,128)(2,1)}) custom-call(bf16[192,128]{1,0:T(8,128)(2,1)} %bitcast.9, bf16[192,128]{1,0:T(8,128)(2,1)} %bitcast.10, bf16[192,128]{1,0:T(8,128)(2,1)} %bitcast.11, bf16[128,3072]{1,0:T(8,128)(2,1)} %weight_hbm.1, ...), custom_call_target="tpu_custom_call" | custom-call | tf_op jit(solution)/shard_map/attention/pallas_call | solution.py:678
  61.6 2.8 %write.1 = (bf16[192,3072]{1,0:T(8,128)(2,1)}, bf16[192,128]{1,0:T(8,128)(2,1)}, bf16[192,128]{1,0:T(8,128)(2,1)}, bf16[192,128]{1,0:T(8,128)(2,1)}, f32[128,3072]{1,0:T(8,128)}) custom-call(bf16[192,3072]{1,0:T(8,128)(2,1)} %get-tuple-element.14.projected, bf16[192,128]{1,0:T(8,128)(2,1)} %get-tuple-element.15.query, ...), custom_call_target="tpu_custom_call" | custom-call | tf_op jit(solution)/shard_map/write/pallas_call | solution.py:763

commit v4 on v3

--- a/solution.py
+++ b/solution.py
@@ -12,9 +12,22 @@
 WIDE = 256
 DIM = 128
 LIMIT = 56 * 2**20
+CHUNKS = 2
+CHUNK = 96 // CHUNKS
 BF16, F32 = jnp.bfloat16, jnp.float32
 ROOT = 1.0 / math.sqrt(DIM)
 SCALE = ROOT * math.log2(math.e)
+
+
+FAR_FIRST = (10, 6, 9, 11, 14, 2, 5, 7, 8, 13, 15, 1, 3, 4, 12)
+
+
+def wrap(index, size):
+    return jnp.where(index >= size, index - size, index)
+
+
+def step(index, bound):
+    return jnp.where(index >= bound, 1, 0)
 
 
 class Place:
@@ -22,13 +35,19 @@
         self.f = lax.axis_index("frame")
         self.h = lax.axis_index("height")
         self.w = lax.axis_index("width")
-        self.xlo = self.f // 2
+        self.xlo = step(self.f, 2)
         self.core = self.f - 2 * self.xlo
-        self.xhi = self.w // 4
+        self.xhi = step(self.w, 4)
         self.y = self.w - 4 * self.xhi
-        self.ring = (2 * self.xhi + self.xlo) * 4 + self.y
         self.sibling = (self.xlo * 2 + 1 - self.core, self.h, self.w)
         self.partner = ((1 - self.xlo) * 2 + self.core, self.h, self.w)
+        x = 2 * self.xhi + self.xlo
+        self.xs = [x] + [wrap(x + d, 4) for d in (1, 2, 3)]
+        self.ys = [self.y] + [wrap(self.y + d, 4) for d in (1, 2, 3)]
+        self.hs = [self.h] + [wrap(self.h + d, 8) for d in range(1, 8)]
+        self.frames = [2 * (at - 2 * step(at, 2)) + self.core for at in self.xs]
+        self.widths = [4 * step(at, 2) for at in self.xs]
+        self.ring = x * 4 + self.y
         self.own_plane = self.core
         self.sib_plane = 1 - self.core
         self.lent_plane = 1 - self.xlo
@@ -37,15 +56,11 @@
         self.hslot = self.h - start(self.h)
         self.wslot = self.w - start(self.w)
 
-    def plane_chip(self, index):
-        x = index // 4
-        y = index - 4 * x
-        xhi = x // 2
-        return ((x - 2 * xhi) * 2 + self.core, self.h, xhi * 4 + y)
+    def plane_chip(self, k):
+        return (self.frames[k // 4], self.h, self.widths[k // 4] + self.ys[k % 4])
 
     def plane_shift(self, k):
-        x = lax.rem(2 * self.xhi + self.xlo + k // 4, 4)
-        return x * 4 + lax.rem(self.y + lax.rem(k, 4), 4)
+        return self.xs[k // 4] * 4 + self.ys[k % 4]
 
 
 def start(index):
@@ -56,7 +71,7 @@
     return (
         (index >= 1, index - 1),
         (index <= 6, index + 1),
-        ((index == 2) | (index == 5), 7 * (index // 5)),
+        ((index == 2) | (index == 5), 7 * step(index, 5)),
     )
 
 
@@ -64,7 +79,7 @@
     return (
         (index >= 1, index - 1),
         (index <= 6, index + 1),
-        ((index == 0) | (index == 7), 2 + 3 * (index // 7)),
+        ((index == 0) | (index == 7), 2 + 3 * step(index, 7)),
     )
 
 
@@ -90,11 +105,11 @@
         pl.semaphore_signal(barrier, inc=1, device_id=target, device_id_type=MESH)
 
     for k in (4, 3, 5, 2, 6):
-        greet((place.f, lax.rem(place.h + k, 8), place.w))
-    for k in (10, 6, 9, 11, 14, 2, 5, 7, 8, 13, 15, 1, 3, 4, 12):
-        greet(place.plane_chip(place.plane_shift(k)))
+        greet((place.f, place.hs[k], place.w))
+    for k in FAR_FIRST:
+        greet(place.plane_chip(k))
     for k in (1, 7):
-        greet((place.f, lax.rem(place.h + k, 8), place.w))
+        greet((place.f, place.hs[k], place.w))
     greet(place.sibling)
 
 
@@ -119,11 +134,7 @@
 
 
 def piece_of(index, chunk):
-    return pl.ds(pl.multiple_of(index * 96 + chunk * 48, 48), 48)
-
-
-def far_first(i):
-    return 1 + lax.rem(i + 9, 15)
+    return pl.ds(pl.multiple_of(index * 96 + chunk * CHUNK, CHUNK), CHUNK)
 
 
 def dot(left, right, over):
@@ -132,12 +143,12 @@
 
 def kernel(
     q_ref, k_ref, v_ref, weight_hbm, grad_hbm,
-    projected_hbm, query_out, kv_out, full,
-    kv, queries, douts, own_prob, own_grad, own_max, lent_prob, lent_grad, lent_max,
-    own_state, lent_state, own_att, lent_att, att_out, att_in, state_out, state_in,
+    projected_hbm, query_out, kv_out, full_hbm,
+    kv, queries, douts, own_prob, own_grad, own_max, their_prob, their_grad, their_max,
+    own_state, their_state, own_att, their_att, att_out, att_in, state_in, att_mine, att_sib,
     stats_out, stats_in, dquery, dquery_out, dquery_in,
-    grads, weight, projected,
-    terms, half, pieces, lines,
+    grads, grads_in, weight, projected,
+    terms, half, pieces, lines, full,
     parts, swap, outgoing, wide, tall, high, side,
     load_sem, store_sem,
     hsend, wsend, ssend, recv, xsend, xrecv,
@@ -149,8 +160,8 @@
     core, ring, h = place.core, place.ring, place.h
     own, sib, lent = place.own_plane * 3, place.sib_plane * 3, place.lent_plane * 3
     kept = 3 - lent
-    hslots = (place.hslot, lax.rem(place.hslot + 1, 3), lax.rem(place.hslot + 2, 3))
-    wslots = (place.wslot, lax.rem(place.wslot + 1, 3), lax.rem(place.wslot + 2, 3))
+    hslots = (place.hslot, wrap(place.hslot + 1, 3), wrap(place.hslot + 2, 3))
+    wslots = (place.wslot, wrap(place.wslot + 1, 3), wrap(place.wslot + 2, 3))
     mine, theirs = pl.ds(0, ROWS), pl.ds(WIDE, ROWS)
 
     greet_all(place)
@@ -164,7 +175,7 @@
     for first in (ROWS, WIDE + ROWS):
         queries[first : first + WIDE - ROWS] = jnp.zeros((WIDE - ROWS, DIM), BF16)
         douts[first : first + WIDE - ROWS] = jnp.zeros((WIDE - ROWS, DIM), BF16)
-    for state, total in ((own_state, own_att), (lent_state, lent_att)):
+    for state, total in ((own_state, own_att), (their_state, their_att)):
         state[...] = jnp.zeros(state.shape, F32)
         state[0:1] = jnp.full((1, state.shape[1]), -jnp.inf, F32)
         total[...] = jnp.zeros(total.shape, F32)
@@ -181,9 +192,16 @@
     query_copy = over(0, queries.at[mine], queries.at[theirs])
     dout_copy = over(1, douts.at[mine], douts.at[theirs])
     att_copy = over(2, att_out, att_in)
-    state_copy = over(3, state_out, state_in)
+    state_copy = over(3, their_state, state_in)
     stats_copy = over(4, stats_out, stats_in)
     dquery_copy = over(5, dquery_out, dquery_in)
+
+    def beside(i, source, target):
+        return remote(source, target, half_sem.at[i], half_sem.at[2 + i], place.sibling)
+
+    their_side = pl.ds(pl.multiple_of((1 - core) * 1536, 1536), 1536)
+    grads_copy = beside(0, grads.at[:, their_side], grads_in)
+    sib_copy = beside(1, att_mine, att_sib)
 
     def window(col, hslot, part):
         return kv.at[col, part, tile_of(hslot)]
@@ -216,11 +234,10 @@
         col = plane + wslot
         arrived(window(col, hslot, part), recv.at[col, hslot, part])
 
-    def forward(plane, tiles, prob, prob_grad, col_max, state, total):
-        width = state.shape[1]
+    def forward(plane, base, first, tiles, prob, prob_grad, col_max, state, total):
         rows = [tile_of(hslot) for _, hslot in tiles]
         scores = [
-            dot(kv[plane + wslot, 0, row], queries[:width], (1, 1))
+            dot(kv[plane + wslot, 0, row], queries[first : first + WIDE], (1, 1))
             for (wslot, _), row in zip(tiles, rows)
         ]
         before = state[0:1]
@@ -229,24 +246,31 @@
             now = jnp.maximum(now, jnp.max(score, axis=0, keepdims=True))
         shrink = jnp.exp2((before - now) * SCALE)
         row_sum = state[1:2] * shrink
-        added = jnp.zeros((DIM, width), F32)
+        added = jnp.zeros((DIM, WIDE), F32)
         for (wslot, hslot), row, score in zip(tiles, rows, scores):
             weights = jnp.exp2((score - now) * SCALE)
             row_sum += jnp.sum(weights, axis=0, keepdims=True)
             values = kv[plane + wslot, 1, row]
-            prob[wslot, row] = weights
-            prob_grad[wslot, row] = dot(values, douts[:width], (1, 1))
-            col_max[wslot, hslot] = now
+            prob[base + wslot, row] = weights
+            prob_grad[base + wslot, row] = dot(values, douts[first : first + WIDE], (1, 1))
+            col_max[base + wslot, hslot] = now
             added += dot(values, weights.astype(BF16), (0, 0))
         state[0:1] = now
         state[1:2] = row_sum
         total[...] = total[...] * shrink + added
 
-    def forward_own(tiles):
-        forward(kept, tiles, own_prob, own_grad, own_max, own_state, own_att)
-
-    def forward_lent(tiles):
-        forward(lent, tiles, lent_prob, lent_grad, lent_max, lent_state, lent_att)
+    def ours(plane, tiles):
+        forward(plane, plane, 0, tiles, own_prob, own_grad, own_max, own_state, own_att)
+
+    def theirs(tiles):
+        forward(
+            lent, 0, WIDE, tiles, their_prob, their_grad, their_max, their_state, their_att
+        )
+
+    def from_sibling(tiles):
+        for wslot, hslot in tiles:
+            for part in range(2):
+                take(sib, wslot, hslot, part)
 
     w0, h0 = wslots[0], hslots[0]
     begin(along_height(w0, 0))
@@ -257,6 +281,7 @@
     begin(to_sibling(w0, h0, 1))
     query_copy.start()
     dout_copy.start()
+    grads_copy.start()
     for wslot, hslot in zip(wslots[1:], hslots[1:]):
         take(own, w0, hslot, 0)
         begin(along_width(hslot, 0))
@@ -269,8 +294,6 @@
         begin(to_sibling(w0, hslot, 1))
         take(own, wslot, h0, 0)
         begin(to_sibling(wslot, h0, 0))
-    query_copy.wait()
-    dout_copy.wait()
     steps = [[(w0, hslot) for hslot in hslots]]
     steps += [[(wslot, hslot) for wslot in wslots[1:]] for hslot in hslots]
 
@@ -280,76 +303,87 @@
                 take(own, wslot, hslot, part)
                 begin(to_sibling(wslot, hslot, part))
 
-    for i in range(4):
-        for wslot, hslot in steps[i]:
-            for part in range(2):
-                take(sib, wslot, hslot, part)
-        if i < 3:
-            forward_lent(steps[i])
-            forward_own(steps[i])
-        if 0 < i < 3:
-            from_corners(steps[i + 1])
-    forward_lent(steps[3])
-    att_out[...] = lent_att[:, WIDE:].astype(BF16)
-    state_out[...] = lent_state[:, WIDE:]
+    ours(own, steps[0])
+    query_copy.wait()
+    dout_copy.wait()
+    from_sibling(steps[0])
+    theirs(steps[0])
+    ours(sib, steps[0])
+    ours(own, steps[1])
+    from_sibling(steps[1])
+    theirs(steps[1])
+    ours(sib, steps[1])
+    from_corners(steps[2])
+    ours(own, steps[2])
+    from_corners(steps[3])
+    from_sibling(steps[2])
+    theirs(steps[2])
+    ours(sib, steps[2])
+    ours(own, steps[3])
+    from_sibling(steps[3])
+    theirs(steps[3])
+    att_out[...] = their_att[...].astype(BF16)
     att_copy.start()
     state_copy.start()
-    forward_own(steps[3])
-
+    ours(sib, steps[3])
+
+    grads_copy.wait()
     att_copy.wait()
     state_copy.wait()
-    shares = [
-        (own_state[...], own_att[...]),
-        (lent_state[:, :WIDE], lent_att[:, :WIDE]),
-        (state_in[...], att_in[...].astype(F32)),
-    ]
-    row_max = jnp.maximum(jnp.maximum(shares[0][0][0:1], shares[1][0][0:1]), shares[2][0][0:1])
-    row_sum = jnp.zeros((1, WIDE), F32)
-    total = jnp.zeros((DIM, WIDE), F32)
-    for state, partial in shares:
-        shrink = jnp.exp2((state[0:1] - row_max) * SCALE)
-        row_sum += state[1:2] * shrink
-        total += partial * shrink
-    inverse = 1.0 / row_sum
-    attended_wide = (total * inverse).astype(BF16)
+    before = own_state[0:1]
+    row_max = jnp.maximum(before, state_in[0:1])
+    shrink = jnp.exp2((before - row_max) * SCALE)
+    shrink_in = jnp.exp2((state_in[0:1] - row_max) * SCALE)
+    inverse = 1.0 / (own_state[1:2] * shrink + state_in[1:2] * shrink_in)
+    attended_wide = (
+        (own_att[...] * shrink + att_in[...].astype(F32) * shrink_in) * inverse
+    ).astype(BF16)
+    att_mine[...] = attended_wide
+    sib_copy.start()
     attended = attended_wide[:, :ROWS]
-
-    def weight_terms(side):
-        def one(i, carry):
-            columns = pl.ds(pl.multiple_of(side * 1536 + i * 512, 512), 512)
-            term = dot(attended, grads[:, columns], (1, 0)).astype(BF16)
-            for j in range(4):
-                rows = pl.ds(pl.multiple_of(i * 512 + j * 128, 128), 128)
-                terms[side, rows] = term[:, j * 128 : (j + 1) * 128]
-            return carry
-
-        lax.fori_loop(0, 3, one, 0)
-
-    half_copy = remote(terms.at[1 - core], half, half_sem.at[0], half_sem.at[1], place.sibling)
-    weight_terms(1 - core)
-    half_copy.start()
     stats_out[0:1] = row_max
     stats_out[1:2] = inverse
     stats_out[2:3] = jnp.sum(
         jnp.transpose(douts[:WIDE].astype(F32)) * attended_wide.astype(F32), axis=0, keepdims=True
     )
     stats_copy.start()
-    weight_terms(core)
-
-    def backward(plane, wslot, prob, prob_grad, col_max, stats):
-        width = prob.shape[2]
-        added = jnp.zeros((DIM, width), F32)
+    for i in range(3):
+        columns = pl.ds(pl.multiple_of(core * 1536 + i * 512, 512), 512)
+        terms[i] = dot(attended, grads[:, columns], (1, 0))
+    sib_copy.wait()
+    for i in range(3):
+        term = terms[i] + dot(
+            att_sib[:, :ROWS], grads_in[:, i * 512 : (i + 1) * 512], (1, 0)
+        )
+        for j in range(4):
+            half[i * 512 + j * 128 : i * 512 + (j + 1) * 128] = term[
+                :, j * 128 : (j + 1) * 128
+            ].astype(BF16)
+
+    def backward(plane, wslot, both):
+        added = jnp.zeros((DIM, 2 * WIDE if both else WIDE), F32)
         for hslot in range(3):
             rows = tile_of(hslot)
-            share = jnp.exp2((col_max[wslot, hslot] - stats[0]) * SCALE) * stats[1]
-            probability = prob[wslot, rows] * share
-            score_grad = (probability * (prob_grad[wslot, rows] - stats[2])).astype(BF16)
-            value_part = dot(probability.astype(BF16), douts[:width], (1, 0))
+            held = [(own_prob, own_grad, own_max, stats_out, plane + wslot)]
+            if both:
+                held.append((their_prob, their_grad, their_max, stats_in, wslot))
+            shares, score_grads = [], []
+            for prob, prob_grad, col_max, stats, col in held:
+                share = jnp.exp2((col_max[col, hslot] - stats[0:1]) * SCALE) * stats[1:2]
+                probability = prob[col, rows] * share
+                shares.append(probability.astype(BF16))
+                score_grads.append(
+                    (probability * (prob_grad[col, rows] - stats[2:3])).astype(BF16)
+                )
+            share = jnp.concatenate(shares, axis=1) if both else shares[0]
+            score_grad = jnp.concatenate(score_grads, axis=1) if both else score_grads[0]
+            width = added.shape[1]
+            value_part = dot(share, douts[:width], (1, 0))
             key_part = dot(score_grad, queries[:width], (1, 0)) * ROOT
             parts[plane + wslot, 1, rows] = value_part.astype(BF16)
             parts[plane + wslot, 0, rows] = key_part.astype(BF16)
             added += dot(kv[plane + wslot, 0, rows], score_grad, (0, 0))
-        dquery[:, :width] += added
+        dquery[:, : added.shape[1]] += added
 
     def swap_copy(wslot):
         return remote(
@@ -358,44 +392,26 @@
         )
 
     def own_column(wslot, carry):
-        stats = [stats_out[i : i + 1] for i in range(3)]
-        backward(kept, wslot, own_prob, own_grad, own_max, stats)
+        backward(kept, wslot, False)
         pl.when(place.lends_own)(swap_copy(wslot).start)
         return carry
-
-    lax.fori_loop(0, 3, own_column, 0)
-
-    half_copy.wait()
 
     def piece_copy(chunk, k):
         to = place.plane_shift(k)
         return remote(
             half.at[piece_of(to, chunk)], pieces.at[chunk, ring], piece_send.at[chunk, to],
-            piece_recv.at[chunk, ring], place.plane_chip(to),
-        )
-
-    def scatter(chunk):
-        def add_half(piece, carry):
-            rows = piece_of(piece, chunk)
-            half[rows] = (terms[core, rows].astype(F32) + half[rows].astype(F32)).astype(BF16)
-            return carry
-
-        def start_piece(i, carry):
-            piece_copy(chunk, far_first(i)).start()
-            return carry
-
-        lax.fori_loop(0, 16, add_half, 0)
-        lax.fori_loop(0, 15, start_piece, 0)
-
-    scatter(0)
-    scatter(1)
+            piece_recv.at[chunk, ring], place.plane_chip(k),
+        )
+
+    for chunk in range(CHUNKS):
+
+        for k in FAR_FIRST:
+            piece_copy(chunk, k).start()
+    lax.fori_loop(0, 3, own_column, 0)
     stats_copy.wait()
 
     def lent_column(wslot, carry):
-        stats = [
-            jnp.concatenate([stats_out[i : i + 1], stats_in[i : i + 1]], axis=1) for i in range(3)
-        ]
-        backward(lent, wslot, lent_prob, lent_grad, lent_max, stats)
+        backward(lent, wslot, True)
         pl.when(place.lends_sib)(swap_copy(wslot).start)
         return carry
 
@@ -450,34 +466,30 @@
         return carry
 
     lax.fori_loop(0, 6, project, 0)
-    store = pltpu.make_async_copy(projected, projected_hbm, store_sem)
+    store = pltpu.make_async_copy(projected, projected_hbm, store_sem.at[0])
     store.start()
     dquery_copy.wait()
     query_out[...] = (jnp.transpose(dquery[:, :WIDE] + dquery_in[...])[:ROWS] * ROOT).astype(BF16)
 
     def line_copy(chunk, k):
-        to = lax.rem(h + k, 8)
+        to = place.hs[k]
         return remote(
             lines.at[chunk, h], lines.at[chunk, h], line_send.at[chunk, to],
             line_recv.at[chunk, h], (place.f, to, place.w),
         )
 
     def exchange(chunk):
-        def add_piece(k, total):
+        total = half[piece_of(ring, chunk)].astype(F32)
+        for k in range(1, 16):
             other = place.plane_shift(k)
             arrived(pieces.at[chunk, other], piece_recv.at[chunk, other])
-            return total + pieces[chunk, other].astype(F32)
-
-        def start_line(k, carry):
+            total = total + pieces[chunk, other].astype(F32)
+        lines[chunk, h] = total.astype(BF16)
+        for k in (4, 3, 5, 2, 6, 1, 7):
             line_copy(chunk, k).start()
-            return carry
-
-        total = lax.fori_loop(1, 16, add_piece, half[piece_of(ring, chunk)].astype(F32))
-        lines[chunk, h] = total.astype(BF16)
-        lax.fori_loop(1, 8, start_line, 0)
         return total
 
-    totals = [exchange(0), exchange(1)]
+    totals = [exchange(chunk) for chunk in range(CHUNKS)]
 
     def add_wide(i, hslot):
         arrived(wide.at[i, hslot], wide_recv.at[i, hslot])
@@ -528,7 +540,7 @@
         rows = piece_of(ring, chunk)
         return remote(
             full.at[core, rows], full.at[core, rows], full_send.at[chunk, to],
-            full_recv.at[core, chunk, ring], place.plane_chip(to),
+            full_recv.at[core, chunk, ring], place.plane_chip(k),
         )
 
     def pass_copy(chunk, piece):
@@ -539,80 +551,25 @@
         )
 
     def spread(chunk):
-        def add_line(k, total):
-            other = lax.rem(h + k, 8)
+        total = totals[chunk]
+        for k in range(1, 8):
+            other = place.hs[k]
             arrived(lines.at[chunk, other], line_recv.at[chunk, other])
-            return total + lines[chunk, other].astype(F32)
-
-        def start_full(i, carry):
-            full_copy(chunk, far_first(i)).start()
-            return carry
-
-        total = lax.fori_loop(1, 8, add_line, totals[chunk])
+            total = total + lines[chunk, other].astype(F32)
         full[core, piece_of(ring, chunk)] = (total * (1.0 / 256.0)).astype(BF16)
-        lax.fori_loop(0, 15, start_full, 0)
+        for k in FAR_FIRST:
+            full_copy(chunk, k).start()
         pass_copy(chunk, ring).start()
 
-    spread(0)
-    spread(1)
-
-    rows = tile_of(place.hslot)
-    for i, (there, _h) in enumerate(neighbours(h)):
-
-        @pl.when(there)
-        def _():
-            arrived(high.at[i], high_recv.at[i])
-            outgoing[place.wslot, 0, rows] += high[i].astype(F32)
-
-    for i, (there, _w) in enumerate(neighbours(place.w)):
-
-        @pl.when(there)
-        def _():
-            arrived(side.at[i], side_recv.at[i])
-            outgoing[place.wslot, 1, rows] += side[i].astype(F32)
-
-    kv_out[...] = outgoing[place.wslot, :, rows].astype(BF16)
-
-    for chunk in range(2):
-
-        def pass_on(k, carry):
-            other = place.plane_shift(k)
-            arrived(full.at[core, piece_of(other, chunk)], full_recv.at[core, chunk, other])
-            pass_copy(chunk, other).start()
-            return carry
-
-        lax.fori_loop(1, 16, pass_on, 0)
-
-    def take_rest(piece, carry):
-        for chunk in range(2):
-            arrived(
-                full.at[1 - core, piece_of(piece, chunk)], full_recv.at[1 - core, chunk, piece]
-            )
-        return carry
-
-    lax.fori_loop(0, 16, take_rest, 0)
-
-    def left_plane(k, carry):
-        for chunk in range(2):
+    for chunk in range(CHUNKS):
+        spread(chunk)
+
+    for chunk in range(CHUNKS):
+        for k in range(1, 16):
             piece_copy(chunk, k).wait_send()
-            full_copy(chunk, k).wait_send()
-        return carry
-
-    lax.fori_loop(1, 16, left_plane, 0)
-
-    def left_line(k, carry):
-        for chunk in range(2):
+        for k in range(1, 8):
             line_copy(chunk, k).wait_send()
-        return carry
-
-    lax.fori_loop(1, 8, left_line, 0)
-
-    def left_pass(piece, carry):
-        for chunk in range(2):
-            pass_copy(chunk, piece).wait_send()
-        return carry
-
-    lax.fori_loop(0, 16, left_pass, 0)
+
     def left_column(slot, carry):
         swap_copy(slot).wait_send()
         for hslot in range(3):
@@ -627,11 +584,65 @@
     finish(along_width(h0, 1))
     for i, (there, to) in enumerate(owners(place.w)):
         pl.when(there)(lambda: three(lambda slot: width_copy(i, to, slot).wait_send()))
+    for i, (there, to) in enumerate(owners(h)):
+        pl.when(there)(lambda: three(lambda slot: tall_copy(i, to, slot).wait_send()))
+
+    rows = tile_of(place.hslot)
+    for i, (there, _h) in enumerate(neighbours(h)):
+
+        @pl.when(there)
+        def _():
+            arrived(high.at[i], high_recv.at[i])
+            outgoing[place.wslot, 0, rows] += high[i].astype(F32)
+
+    for i, (there, _w) in enumerate(neighbours(place.w)):
+
+        @pl.when(there)
+        def _():
+            arrived(side.at[i], side_recv.at[i])
+            outgoing[place.wslot, 1, rows] += side[i].astype(F32)
+
+    kv_out[...] = outgoing[place.wslot, :, rows].astype(BF16)
+
+    for chunk in range(CHUNKS):
+
+        for k in range(1, 16):
+            other = place.plane_shift(k)
+            arrived(full.at[core, piece_of(other, chunk)], full_recv.at[core, chunk, other])
+            pass_copy(chunk, other).start()
+    store_half = pltpu.make_async_copy(full.at[core], full_hbm.at[core], store_sem.at[1])
+    store_half.start()
+
+    def take_rest(piece, carry):
+        for chunk in range(CHUNKS):
+            arrived(
+                full.at[1 - core, piece_of(piece, chunk)], full_recv.at[1 - core, chunk, piece]
+            )
+        return carry
+
+    lax.fori_loop(0, 16, take_rest, 0)
+    store_rest = pltpu.make_async_copy(
+        full.at[1 - core], full_hbm.at[1 - core], store_sem.at[2]
+    )
+    store_rest.start()
+
+    for chunk in range(CHUNKS):
+        for k in range(1, 16):
+            full_copy(chunk, k).wait_send()
+
+    def left_pass(piece, carry):
+        for chunk in range(CHUNKS):
+            pass_copy(chunk, piece).wait_send()
+        return carry
+
+    lax.fori_loop(0, 16, left_pass, 0)
+    for i, (there, to) in enumerate(owners(place.w)):
         pl.when(there)(side_copy(i, to).wait_send)
     for i, (there, to) in enumerate(owners(h)):
-        pl.when(there)(lambda: three(lambda slot: tall_copy(i, to, slot).wait_send()))
         pl.when(there)(height_copy(i, to).wait_send)
     store.wait()
+    store_half.wait()
+    store_rest.wait()
 
 
 def write_kernel(
@@ -684,37 +695,40 @@
             jax.ShapeDtypeStruct((2, 1536, DIM), BF16),
         ),
         in_specs=[here, here, here, there, there],
-        out_specs=[there, here, here, here],
+        out_specs=[there, here, here, there],
         scratch_shapes=[
             vmem((6,) + column, BF16),
             vmem((2 * WIDE, DIM), BF16),
             vmem((2 * WIDE, DIM), BF16),
+            vmem((6, 3 * ROWS, WIDE), F32),
+            vmem((6, 3 * ROWS, WIDE), F32),
+            vmem((6, 3, 1, WIDE), F32),
             vmem((3, 3 * ROWS, WIDE), F32),
             vmem((3, 3 * ROWS, WIDE), F32),
             vmem((3, 3, 1, WIDE), F32),
-            vmem((3, 3 * ROWS, 2 * WIDE), F32),
-            vmem((3, 3 * ROWS, 2 * WIDE), F32),
-            vmem((3, 3, 1, 2 * WIDE), F32),
             vmem((8, WIDE), F32),
-            vmem((8, 2 * WIDE), F32),
+            vmem((8, WIDE), F32),
             vmem((DIM, WIDE), F32),
-            vmem((DIM, 2 * WIDE), F32),
+            vmem((DIM, WIDE), F32),
             vmem((DIM, WIDE), BF16),
             vmem((DIM, WIDE), BF16),
             vmem((8, WIDE), F32),
-            vmem((8, WIDE), F32),
+            vmem((DIM, WIDE), BF16),
+            vmem((DIM, WIDE), BF16),
             vmem((8, WIDE), F32),
             vmem((8, WIDE), F32),
             vmem((DIM, 2 * WIDE), F32),
             vmem((DIM, WIDE), F32),
             vmem((DIM, WIDE), F32),
             vmem((ROWS, model), BF16),
+            vmem((ROWS, 1536), BF16),
             vmem((DIM, model), BF16),
             vmem((ROWS, model), BF16),
+            vmem((3, DIM, 512), F32),
+            vmem((1536, DIM), BF16),
+            vmem((CHUNKS, 16, CHUNK, DIM), BF16),
+            vmem((CHUNKS, 8, CHUNK, DIM), BF16),
             vmem((2, 1536, DIM), BF16),
-            vmem((1536, DIM), BF16),
-            vmem((2, 16, 48, DIM), BF16),
-            vmem((2, 8, 48, DIM), BF16),
             vmem((6,) + column, BF16),
             vmem((3,) + column, BF16),
             vmem((3,) + column, F32),
@@ -723,21 +737,21 @@
             vmem((3,) + tile, BF16),
             vmem((3,) + tile, BF16),
             dma((2,)),
-            dma,
+            dma((3,)),
             dma((3, 3, 2)),
             dma((3, 3, 2)),
             dma((3, 3, 2)),
             dma((6, 3, 2)),
             dma((6,)),
             dma((6,)),
-            dma((2,)),
-            dma((2, 16)),
-            dma((2, 16)),
-            dma((2, 8)),
-            dma((2, 8)),
-            dma((2, 16)),
-            dma((2, 16)),
-            dma((2, 2, 16)),
+            dma((4,)),
+            dma((CHUNKS, 16)),
+            dma((CHUNKS, 16)),
+            dma((CHUNKS, 8)),
+            dma((CHUNKS, 8)),
+            dma((CHUNKS, 16)),
+            dma((CHUNKS, 16)),
+            dma((2, CHUNKS, 16)),
             dma((3,)),
             dma((3,)),
             dma((3, 3)),

time: 64.6 us -> 61.1 us (0.946)
  Pallas kernels: 63.7 us -> 60.3 us
    pallas_call x1, Pallas kernels: 60.9 us -> 57.5 us  [body(): pl.pallas_call(kernel, out_shape=(jax.ShapeDtypeStruct((ROWS, model), BF1...]
where the time goes in v4:
time: 61.1 us; the launch traced here: 60.9 us
  Pallas kernels  60.3 us (99%)
  between operations  0.64 us (1%)
    pallas_call x1, Pallas kernels, body(): pl.pallas_call(kernel, out_shape=(jax.ShapeDtypeStruct((ROWS, model), BF1...  57.5 us
    pallas_call x1, Pallas kernels, body(): pl.pallas_call(write_kernel, out_shape=(jax.ShapeDtypeStruct((ROWS, model...  2.8 us

profile of v4, /device:TPU:1, one launch (start us, length us, event | category | flops | bytes accessed | tf_op | source)
XLA Modules:
  0.0 60.9 jit_solution(11358666120482816371)
XLA Ops:
  0.6 57.5 %attention.1 = (bf16[192,3072]{1,0:T(8,128)(2,1)}, bf16[192,128]{1,0:T(8,128)(2,1)}, bf16[2,192,128]{2,1,0:T(8,128)(2,1)}, bf16[2,1536,128]{2,1,0:T(8,128)(2,1)}) custom-call(bf16[192,128]{1,0:T(8,128)(2,1)} %bitcast.9, bf16[192,128]{1,0:T(8,128)(2,1)} %bitcast.10, bf16[192,128]{1,0:T(8,128)(2,1)} %bitcast.11, bf16[128,3072]{1,0:T(8,128)(2,1)} %weight_hbm.1, ...), custom_call_target="tpu_custom_call" | custom-call | tf_op jit(solution)/shard_map/attention/pallas_call | solution.py:689
  58.1 2.8 %write.1 = (bf16[192,3072]{1,0:T(8,128)(2,1)}, bf16[192,128]{1,0:T(8,128)(2,1)}, bf16[192,128]{1,0:T(8,128)(2,1)}, bf16[192,128]{1,0:T(8,128)(2,1)}, f32[128,3072]{1,0:T(8,128)}) custom-call(bf16[192,3072]{1,0:T(8,128)(2,1)} %get-tuple-element.14.projected, bf16[192,128]{1,0:T(8,128)(2,1)} %get-tuple-element.15.query, ...), custom_call_target="tpu_custom_call" | custom-call | tf_op jit(solution)/shard_map/write/pallas_call | solution.py:777

commit v5 on v4

--- a/solution.py
+++ b/solution.py
@@ -134,7 +134,11 @@
 
 
 def piece_of(index, chunk):
-    return pl.ds(pl.multiple_of(index * 96 + chunk * CHUNK, CHUNK), CHUNK)
+    return pl.ds(pl.multiple_of((chunk * 16 + index) * CHUNK, CHUNK), CHUNK)
+
+
+def group_of(index, chunk):
+    return pl.ds(pl.multiple_of((chunk * 16 + index * 4) * CHUNK, 4 * CHUNK), 4 * CHUNK)
 
 
 def dot(left, right, over):
@@ -152,7 +156,7 @@
     parts, swap, outgoing, wide, tall, high, side,
     load_sem, store_sem,
     hsend, wsend, ssend, recv, xsend, xrecv,
-    half_sem, piece_send, piece_recv, line_send, line_recv, full_send, pass_send, full_recv,
+    half_sem, piece_send, piece_recv, line_send, line_recv, full_send, pass_send, pass_recv, full_recv,
     swap_send, swap_recv, wide_send, wide_recv, tall_send, tall_recv,
     high_send, high_recv, side_send, side_recv,
 ):
@@ -468,9 +472,6 @@
     lax.fori_loop(0, 6, project, 0)
     store = pltpu.make_async_copy(projected, projected_hbm, store_sem.at[0])
     store.start()
-    dquery_copy.wait()
-    query_out[...] = (jnp.transpose(dquery[:, :WIDE] + dquery_in[...])[:ROWS] * ROOT).astype(BF16)
-
     def line_copy(chunk, k):
         to = place.hs[k]
         return remote(
@@ -491,63 +492,19 @@
 
     totals = [exchange(chunk) for chunk in range(CHUNKS)]
 
-    def add_wide(i, hslot):
-        arrived(wide.at[i, hslot], wide_recv.at[i, hslot])
-        outgoing[place.wslot, 0, tile_of(hslot)] += wide[i, hslot].astype(F32)
-
-    def add_tall(i, wslot):
-        arrived(tall.at[i, wslot], tall_recv.at[i, wslot])
-        outgoing[wslot, 1, tile_of(place.hslot)] += tall[i, wslot].astype(F32)
-
-    for i, (there, _w) in enumerate(neighbours(place.w)):
-        pl.when(there)(lambda: three(lambda slot: add_wide(i, slot)))
-    for i, (there, _h) in enumerate(neighbours(h)):
-        pl.when(there)(lambda: three(lambda slot: add_tall(i, slot)))
-
-    def height_copy(i, to):
-        rows = tile_of(to - start(h))
-        return remote(
-            swap.at[place.wslot, 0, rows], high.at[back[i]], high_send.at[i],
-            high_recv.at[back[i]], (place.f, to, place.w),
-        )
-
-    def side_copy(i, to):
-        rows = tile_of(place.hslot)
-        return remote(
-            swap.at[to - start(place.w), 1, rows], side.at[back[i]], side_send.at[i],
-            side_recv.at[back[i]], (place.f, h, to),
-        )
-
-    for i, (there, to) in enumerate(owners(h)):
-
-        @pl.when(there)
-        def _():
-            rows = tile_of(to - start(h))
-            swap[place.wslot, 0, rows] = outgoing[place.wslot, 0, rows].astype(BF16)
-            height_copy(i, to).start()
-
-    for i, (there, to) in enumerate(owners(place.w)):
-
-        @pl.when(there)
-        def _():
-            rows = tile_of(place.hslot)
-            wslot = to - start(place.w)
-            swap[wslot, 1, rows] = outgoing[wslot, 1, rows].astype(BF16)
-            side_copy(i, to).start()
-
     def full_copy(chunk, k):
         to = place.plane_shift(k)
         rows = piece_of(ring, chunk)
         return remote(
             full.at[core, rows], full.at[core, rows], full_send.at[chunk, to],
-            full_recv.at[core, chunk, ring], place.plane_chip(k),
-        )
-
-    def pass_copy(chunk, piece):
-        rows = piece_of(piece, chunk)
+            full_recv.at[chunk, ring], place.plane_chip(k),
+        )
+
+    def pass_copy(chunk, group):
+        rows = group_of(group, chunk)
         return remote(
-            full.at[core, rows], full.at[core, rows], pass_send.at[chunk, piece],
-            full_recv.at[core, chunk, piece], place.sibling,
+            full.at[core, rows], full.at[core, rows], pass_send.at[chunk, group],
+            pass_recv.at[chunk, group], place.sibling,
         )
 
     def spread(chunk):
@@ -559,10 +516,58 @@
         full[core, piece_of(ring, chunk)] = (total * (1.0 / 256.0)).astype(BF16)
         for k in FAR_FIRST:
             full_copy(chunk, k).start()
-        pass_copy(chunk, ring).start()
-
-    for chunk in range(CHUNKS):
+
+    spread(0)
+
+    def add_wide(i, hslot):
+        arrived(wide.at[i, hslot], wide_recv.at[i, hslot])
+        outgoing[place.wslot, 0, tile_of(hslot)] += wide[i, hslot].astype(F32)
+
+    def add_tall(i, wslot):
+        arrived(tall.at[i, wslot], tall_recv.at[i, wslot])
+        outgoing[wslot, 1, tile_of(place.hslot)] += tall[i, wslot].astype(F32)
+
+    for i, (there, _w) in enumerate(neighbours(place.w)):
+        pl.when(there)(lambda: three(lambda slot: add_wide(i, slot)))
+    for i, (there, _h) in enumerate(neighbours(h)):
+        pl.when(there)(lambda: three(lambda slot: add_tall(i, slot)))
+
+    def height_copy(i, to):
+        rows = tile_of(to - start(h))
+        return remote(
+            swap.at[place.wslot, 0, rows], high.at[back[i]], high_send.at[i],
+            high_recv.at[back[i]], (place.f, to, place.w),
+        )
+
+    def side_copy(i, to):
+        rows = tile_of(place.hslot)
+        return remote(
+            swap.at[to - start(place.w), 1, rows], side.at[back[i]], side_send.at[i],
+            side_recv.at[back[i]], (place.f, h, to),
+        )
+
+    for i, (there, to) in enumerate(owners(h)):
+
+        @pl.when(there)
+        def _():
+            rows = tile_of(to - start(h))
+            swap[place.wslot, 0, rows] = outgoing[place.wslot, 0, rows].astype(BF16)
+            height_copy(i, to).start()
+
+    for i, (there, to) in enumerate(owners(place.w)):
+
+        @pl.when(there)
+        def _():
+            rows = tile_of(place.hslot)
+            wslot = to - start(place.w)
+            swap[wslot, 1, rows] = outgoing[wslot, 1, rows].astype(BF16)
+            side_copy(i, to).start()
+
+    for chunk in range(1, CHUNKS):
         spread(chunk)
+    dquery_copy.wait()
+    query_out[...] = (jnp.transpose(dquery[:, :WIDE] + dquery_in[...])[:ROWS] * ROOT).astype(BF16)
+
 
     for chunk in range(CHUNKS):
         for k in range(1, 16):
@@ -606,21 +611,18 @@
 
     for chunk in range(CHUNKS):
 
-        for k in range(1, 16):
-            other = place.plane_shift(k)
-            arrived(full.at[core, piece_of(other, chunk)], full_recv.at[core, chunk, other])
-            pass_copy(chunk, other).start()
+        for group in range(4):
+            for k in range(4 * group, 4 * group + 4):
+                if k:
+                    other = place.plane_shift(k)
+                    arrived(full.at[core, piece_of(other, chunk)], full_recv.at[chunk, other])
+            pass_copy(chunk, place.xs[group]).start()
     store_half = pltpu.make_async_copy(full.at[core], full_hbm.at[core], store_sem.at[1])
     store_half.start()
 
-    def take_rest(piece, carry):
-        for chunk in range(CHUNKS):
-            arrived(
-                full.at[1 - core, piece_of(piece, chunk)], full_recv.at[1 - core, chunk, piece]
-            )
-        return carry
-
-    lax.fori_loop(0, 16, take_rest, 0)
+    for chunk in range(CHUNKS):
+        for group in range(4):
+            arrived(full.at[1 - core, group_of(group, chunk)], pass_recv.at[chunk, group])
     store_rest = pltpu.make_async_copy(
         full.at[1 - core], full_hbm.at[1 - core], store_sem.at[2]
     )
@@ -630,12 +632,9 @@
         for k in range(1, 16):
             full_copy(chunk, k).wait_send()
 
-    def left_pass(piece, carry):
-        for chunk in range(CHUNKS):
-            pass_copy(chunk, piece).wait_send()
-        return carry
-
-    lax.fori_loop(0, 16, left_pass, 0)
+    for chunk in range(CHUNKS):
+        for group in range(4):
+            pass_copy(chunk, group).wait_send()
     for i, (there, to) in enumerate(owners(place.w)):
         pl.when(there)(side_copy(i, to).wait_send)
     for i, (there, to) in enumerate(owners(h)):
@@ -750,8 +749,9 @@
             dma((CHUNKS, 8)),
             dma((CHUNKS, 8)),
             dma((CHUNKS, 16)),
+            dma((CHUNKS, 4)),
+            dma((CHUNKS, 4)),
             dma((CHUNKS, 16)),
-            dma((2, CHUNKS, 16)),
             dma((3,)),
             dma((3,)),
             dma((3, 3)),

time: 61.1 us -> 59.8 us (0.979)
  the two profiles are of different devices: /device:TPU:1 before, /device:TPU:33 now
where the time goes in v5:
time: 59.8 us; the launch traced here: 59.6 us
  Pallas kernels  58.9 us (98%)
  between operations  0.64 us (1%)
    pallas_call x1, Pallas kernels, body(): pl.pallas_call(kernel, out_shape=(jax.ShapeDtypeStruct((ROWS, model), BF1...  56.1 us
    pallas_call x1, Pallas kernels, body(): pl.pallas_call(write_kernel, out_shape=(jax.ShapeDtypeStruct((ROWS, model...  2.8 us

profile of v5, /device:TPU:33, one launch (start us, length us, event | category | flops | bytes accessed | tf_op | source)
XLA Modules:
  0.0 59.6 jit_solution(2105459699782614508)
XLA Ops:
  0.6 56.1 %attention.1 = (bf16[192,3072]{1,0:T(8,128)(2,1)}, bf16[192,128]{1,0:T(8,128)(2,1)}, bf16[2,192,128]{2,1,0:T(8,128)(2,1)}, bf16[2,1536,128]{2,1,0:T(8,128)(2,1)}) custom-call(bf16[192,128]{1,0:T(8,128)(2,1)} %bitcast.9, bf16[192,128]{1,0:T(8,128)(2,1)} %bitcast.10, bf16[192,128]{1,0:T(8,128)(2,1)} %bitcast.11, bf16[128,3072]{1,0:T(8,128)(2,1)} %weight_hbm.1, ...), custom_call_target="tpu_custom_call" | custom-call | tf_op jit(solution)/shard_map/attention/pallas_call | solution.py:688
  56.8 2.8 %write.1 = (bf16[192,3072]{1,0:T(8,128)(2,1)}, bf16[192,128]{1,0:T(8,128)(2,1)}, bf16[192,128]{1,0:T(8,128)(2,1)}, bf16[192,128]{1,0:T(8,128)(2,1)}, f32[128,3072]{1,0:T(8,128)}) custom-call(bf16[192,3072]{1,0:T(8,128)(2,1)} %get-tuple-element.14.projected, bf16[192,128]{1,0:T(8,128)(2,1)} %get-tuple-element.15.query, ...), custom_call_target="tpu_custom_call" | custom-call | tf_op jit(solution)/shard_map/write/pallas_call | solution.py:777
